TPU v7x, 32 devices: a whole 2x2x4 slice. The times are simulated.
32 devices in a mesh: pipe: 4 (over y, core), ctx: 4 (over z), tp: 2 (over x).
Axes of the slice: x: 2, y: 2, z: 4, core: 2. Of those that a mesh axis runs over, the one named last changes fastest.
Arguments:
- queries: bfloat16 [4, 512, 32, 128], P('pipe', 'ctx', 'tp'), may hold values from -45 to 45
- key_value: bfloat16 [4, 2, 512, 8, 128], P('pipe', None, 'ctx', 'tp'), may hold values from -6 to 6
- mamba_in: bfloat16 [4, 512, 8192], P('pipe', 'ctx', 'tp'), may hold values from -6 to 6
- gate_in: bfloat16 [4, 512, 8192], P('pipe', 'ctx', 'tp'), may hold values from -6 to 6
- step_low: bfloat16 [4, 512, 512], P('pipe', 'ctx'), may hold values from -3 to 3
- step_weight: bfloat16 [4, 512, 8192], P('pipe', None, 'tp'), may hold values from -0.25 to 0.25
- step_bias: float32 [4, 8192], P('pipe', 'tp'), may hold values from -4.6 to -3.2
- decay_rate: float32 [4, 8, 8192], P('pipe', None, 'tp'), may hold values from 0.048828125 to 2.5
- conv_weight: float32 [4, 4, 8192], P('pipe', None, 'tp'), may hold values from -3 to 3
- conv_bias: float32 [4, 8192], P('pipe', 'tp'), may hold values from -3 to 3
- state_weight: bfloat16 [4, 8192, 16], P('pipe', 'tp'), may hold values from -0.0625 to 0.0625
- skip_gain: float32 [4, 8192], P('pipe', 'tp'), may hold values from 0.5 to 1.5
Outputs:
- attended: bfloat16 [4, 512, 32, 128], P('pipe', 'ctx', 'tp')
- mamba_out: bfloat16 [4, 512, 8192], P('pipe', 'ctx', 'tp')
All inputs are finite; a program needn't handle non-finite values.
Results may differ from a plain program's by a relative error of at most 0.023.
Values may be sent and summed in bfloat16 or wider, within the bound.
A program may use at most 64 MiB of HBM per device.

v0:
```python
import math

import jax
import jax.numpy as jnp
from jax import lax
from jax.sharding import PartitionSpec as P


def passed_along(value, axis, steps):
    count = lax.axis_size(axis)
    leading, last = (max(0, -steps), min(count, count - steps))
    return lax.ppermute(value, axis, [(source, source + steps) for source in range(leading, last)])


def prefix(x, axis, join, neutral):
    place = lax.axis_index(axis)
    gathered = jax.tree.map(
        lambda a, kind: lax.all_gather(a.astype(kind), axis), x, (jnp.bfloat16, jnp.bfloat16)
    )
    state = jax.tree.map(lambda a, e: jnp.zeros_like(a) + jnp.asarray(e, a.dtype), x, neutral)

    def one(hop, state):
        return join(
            state,
            jax.tree.map(
                lambda a, own: lax.dynamic_index_in_dim(a, hop, 0, False).astype(own.dtype),
                gathered,
                x,
            ),
        )

    return lax.fori_loop(0, place, one, state)


def passed_along_2(block, axis, distance):
    devices = range(lax.axis_size(axis))
    route = [((i - distance) % len(devices), i) for i in devices]
    return lax.ppermute(block, axis, route)


def empty_state(kv_count, group_size, query_rows, head_width):
    return (
        jnp.full((kv_count, group_size, query_rows), -1e30, jnp.float32),
        jnp.zeros((kv_count, group_size, query_rows), jnp.float32),
        jnp.zeros((kv_count, group_size, query_rows, head_width), jnp.float32),
    )


def absorb(softmax_state, query_block, query_pos, kv_piece, key_pos):

    def compute(current):
        running_max, running_sum, weighted = current
        scores = jnp.einsum(
            "tkgd,skd->kgts", query_block, kv_piece[0], preferred_element_type=jnp.float32
        ) / math.sqrt(query_block.shape[-1])
        allowed = key_pos[None, :] <= query_pos[:, None]
        new_max = jnp.maximum(running_max, jnp.max(jnp.where(allowed, scores, -1e30), axis=-1))
        weights = jnp.where(allowed, jnp.exp(scores - new_max[..., None]), 0.0)
        running_sum = jnp.sum(weights, axis=-1)
        weighted = jnp.einsum(
            "kgts,skd->kgtd",
            weights.astype(jnp.bfloat16),
            kv_piece[1],
            preferred_element_type=jnp.float32,
        )
        return (new_max, running_sum, weighted)

    def unchanged(current):
        return current

    return lax.cond(key_pos[0] <= query_pos[-1], compute, unchanged, softmax_state)


def finish(softmax_state):
    weighted = softmax_state[2] / softmax_state[1][..., None]
    kv_count, group_size, query_rows, head_width = weighted.shape
    return (
        jnp.transpose(weighted, (2, 0, 1, 3))
        .reshape(query_rows, kv_count * group_size, head_width)
        .astype(jnp.bfloat16)
    )


def attend(queries, key_value):
    tok_rows, head_count, head_width = queries.shape
    kv_count = key_value.shape[2]
    group_size = head_count // kv_count
    ctx_index = lax.axis_index("ctx")
    half_rows = tok_rows // 2
    upper_query = queries[half_rows:]
    lower_pos = ctx_index * tok_rows + jnp.arange(half_rows, dtype=jnp.int32)
    upper_pos = ctx_index * tok_rows + half_rows + jnp.arange(tok_rows - half_rows, dtype=jnp.int32)
    lower_query = queries[:half_rows].reshape(half_rows, kv_count, group_size, head_width)
    upper_block = upper_query.reshape(tok_rows - half_rows, kv_count, group_size, head_width)
    initial = (
        empty_state(kv_count, group_size, half_rows, head_width),
        empty_state(kv_count, group_size, tok_rows - half_rows, head_width),
    )
    kv_piece = lax.all_gather(key_value, "ctx", axis=1, tiled=True)
    key_pos = jnp.arange(kv_piece.shape[1], dtype=jnp.int32)
    lower_out = finish(absorb(initial[0], lower_query, lower_pos, kv_piece, key_pos))
    upper_out = finish(absorb(initial[1], upper_block, upper_pos, kv_piece, key_pos))
    return jnp.concatenate([lower_out, upper_out], axis=0)


def mamba_layer(
    mamba_in,
    gate_in,
    step_low,
    step_weight,
    step_bias,
    decay_rate,
    conv_weight,
    conv_bias,
    state_weight,
    skip_gain,
):
    tok_rows, channels = mamba_in.shape
    state_count = decay_rate.shape[0]
    taps = conv_weight.shape[0]
    earlier_rows = passed_along(mamba_in[tok_rows - (taps - 1) :], "ctx", 1)
    padded = jnp.concatenate([earlier_rows, mamba_in], axis=0).astype(jnp.float32)
    conv_out = conv_bias[None, :]
    for tap_index in range(taps):
        conv_out = (
            conv_out + conv_weight[tap_index][None, :] * padded[tap_index : tap_index + tok_rows]
        )
    inner_act = jax.nn.silu(conv_out).astype(jnp.bfloat16)
    entry_read = lax.psum(
        jnp.dot(inner_act, state_weight, preferred_element_type=jnp.float32), "tp"
    )
    entry_map = entry_read[:, :state_count]
    read_map = entry_read[:, state_count:]
    step_size = jax.nn.softplus(
        jnp.dot(step_low, step_weight, preferred_element_type=jnp.float32) + step_bias[None, :]
    )
    drive_input = step_size * inner_act.astype(jnp.float32)
    block_len = min(16, tok_rows)
    block_total = tok_rows // block_len

    def run_block(carry_state, block_rows):
        step_rows, drive_rows, entry_rows, read_rows = block_rows
        outputs = []
        for offset in range(block_len):
            carry_state = (
                jnp.exp(-decay_rate * step_rows[offset][None, :]) * carry_state
                + entry_rows[offset][:, None] * drive_rows[offset][None, :]
            )
            outputs.append(jnp.sum(read_rows[offset][:, None] * carry_state, axis=0))
        return (carry_state, jnp.stack(outputs))

    def blocked(array):
        return array.reshape((block_total, block_len) + array.shape[1:])

    local_state, local_out = lax.scan(
        run_block,
        jnp.zeros((state_count, channels), jnp.float32),
        (blocked(step_size), blocked(drive_input), blocked(entry_map), blocked(read_map)),
    )
    elapsed = jnp.cumsum(step_size, axis=0)
    decay_total = jnp.exp(-decay_rate * elapsed[-1][None, :])

    def combine(earlier, later):
        return (earlier[0] * later[0], earlier[1] * later[0] + later[1])

    carried = prefix(
        (decay_total, local_state),
        "ctx",
        combine,
        (jnp.ones_like(decay_total), jnp.zeros_like(local_state)),
    )
    entering = carried[1]
    carried_in = jnp.sum(
        read_map[:, :, None] * jnp.exp(-decay_rate[None] * elapsed[:, None, :]) * entering[None],
        axis=1,
    )
    scan_out = (
        local_out.reshape(tok_rows, channels)
        + carried_in
        + skip_gain[None, :] * inner_act.astype(jnp.float32)
    )
    return (scan_out * jax.nn.silu(gate_in.astype(jnp.float32))).astype(jnp.bfloat16)


def per_device(
    queries,
    key_value,
    mamba_in,
    gate_in,
    step_low,
    step_weight,
    step_bias,
    decay_rate,
    conv_weight,
    conv_bias,
    state_weight,
    skip_gain,
):
    mixed = attend(queries[0], key_value[0])
    gated = mamba_layer(
        mamba_in[0],
        gate_in[0],
        step_low[0],
        step_weight[0],
        step_bias[0],
        decay_rate[0],
        conv_weight[0],
        conv_bias[0],
        state_weight[0],
        skip_gain[0],
    )
    arrived = passed_along_2((mixed, gated), "pipe", 1)
    return (arrived[0][None], arrived[1][None])


def solution(mesh):
    return jax.shard_map(
        per_device,
        mesh=mesh,
        in_specs=(
            P("pipe", "ctx", "tp", None),
            P("pipe", None, "ctx", "tp", None),
            P("pipe", "ctx", "tp"),
            P("pipe", "ctx", "tp"),
            P("pipe", "ctx", None),
            P("pipe", None, "tp"),
            P("pipe", "tp"),
            P("pipe", None, "tp"),
            P("pipe", None, "tp"),
            P("pipe", "tp"),
            P("pipe", "tp", None),
            P("pipe", "tp"),
        ),
        out_specs=(P("pipe", "ctx", "tp", None), P("pipe", "ctx", "tp")),
        check_vma=False,
    )
```

profile of v0, /device:TPU:0, one launch (start us, length us, event | category | flops | bytes accessed | tf_op | source)
XLA Modules:
  0.0 155.0 jit_solution(17307119553318280460)
XLA Ops:
  8.1 4.9 %collective-permute-start.1 = (bf16[3,4096]{1,0:T(4,128)(2,1)S(1)}, bf16[3,4096]{1,0:T(4,128)(2,1)S(1)}, u32[]{:S(2)}, u32[]{:S(2)}) collective-permute-start(bf16[3,4096]{1,0:T(4,128)(2,1)S(1)} %slice_bitcast_fusion), channel_id=1, source_target_pairs={{0,2},{2,4},{4,6},{1,3},{3,5},{5,7},{8,10},{10,12},{12,14},{9,11},... | collective-permute-start | bytes 73736 | tf_op jit(solution)/shard_map/ppermute | solution.py:12
  13.1 1.7 %copy.30 = bf16[1,2,128,4,128]{4,2,3,1,0:T(8,128)(2,1)} copy(bf16[1,2,128,4,128]{4,3,2,1,0:T(4,128)(2,1)} %param.21) | data formatting | bytes 524288 | tf_op args[1]
  22.5 6.7 %convert_multiply_fusion.3 = (f32[128,4096]{1,0:T(8,128)}, bf16[128,4096]{1,0:T(8,128)(2,1)S(1)}, f32[128,4096]{1,0:T(8,128)S(1)}) fusion(f32[131,4096]{1,0:T(8,128)S(1)} %maximum_convert_fusion, f32[4096]{0:T(1024)S(1)} %bitcast.418, f32[4096]{0:T(1024)S(1)} %bitcast.419, f32[4096]{0:T(1024)S(1)} %bitcast.417, f32[4096]{0:T(1024)S(1)} %bitcast.416, ...), kind=kOutput, calls=%fused_computation.181 | convolution fusion | flops 548405248 | bytes 18055168 | tf_op jit(solution)/shard_map/dot_general | solution.py:135
  29.3 3.1 %reduce_window_sum.11 = f32[128,4096]{1,0:T(8,128)} reduce-window(f32[128,4096]{1,0:T(8,128)S(1)} %get-tuple-element.415, f32[]{:T(128)} %constant.87.clone.1), window={size=128x1 pad=127_0x0_0}, to_apply=%region_27.28 | reduce-window | flops 66584576 | bytes 4194308 | tf_op jit(solution)/shard_map/jit(cumsum)/reduce_window_sum | solution.py:160
  34.3 5.1 %psum.7 = f32[128,16]{0,1:T(8,128)S(1)} all-reduce(f32[128,16]{0,1:T(8,128)} %fusion.84), channel_id=1, replica_groups=mesh['pipe'=4,'ctx'=4,'tp'=2] {'tp'}, use_global_device_ids=true, to_apply=%region_8.9 | all-reduce | flops 2048 | bytes 16384 | tf_op jit(solution)/shard_map/psum | solution.py:129
  40.5 45.0 %while.28 = (s32[]{:T(128)}, f32[8,4096]{1,0:T(8,128)S(1)}, f32[8,16,4096]{2,1,0:T(8,128)}, f32[8,16,4096]{2,1,0:T(8,128)S(1)}, f32[8,4096]{1,0:T(8,128)S(1)}, /...) while((s32[]{:T(128)}, f32[8,4096]{1,0:T(8,128)S(1)}, ...), condition=%wide.region_26.27_spmd.clone, body=%wide.region_9.26_spmd.clone.sunk | while | flops 4194322 | bytes 6164764 | solution.py:155
  40.5 2.5 %constant_dynamic-slice_fusion.65 = (f32[1,1,4096]{2,1,0:T(1,128)S(1)}, f32[1,1,4096]{2,1,0:T(1,128)S(1)}, f32[1,1,4096]{2,1,0:T(1,128)S(1)}, f32[1,1,4096]{2,1,...) fusion(f32[8,16,4096]{2,1,0:T(8,128)} %get-tuple-element.737, ...), kind=kLoop, calls=%fused_computation.121.clone.1 | loop fusion | bytes 1048640 | tf_op jit(solution)/shard_map/while/body/eval_jaxpr/slice | solution.py:147
  45.9 2.7 %constant_dynamic-slice_fusion.65 = (f32[1,1,4096]{2,1,0:T(1,128)S(1)}, f32[1,1,4096]{2,1,0:T(1,128)S(1)}, f32[1,1,4096]{2,1,0:T(1,128)S(1)}, f32[1,1,4096]{2,1,...) fusion(f32[8,16,4096]{2,1,0:T(8,128)} %get-tuple-element.737, ...), kind=kLoop, calls=%fused_computation.121.clone.1 | loop fusion | bytes 1048640 | tf_op jit(solution)/shard_map/while/body/eval_jaxpr/slice | solution.py:147
  51.5 2.8 %constant_dynamic-slice_fusion.65 = (f32[1,1,4096]{2,1,0:T(1,128)S(1)}, f32[1,1,4096]{2,1,0:T(1,128)S(1)}, f32[1,1,4096]{2,1,0:T(1,128)S(1)}, f32[1,1,4096]{2,1,...) fusion(f32[8,16,4096]{2,1,0:T(8,128)} %get-tuple-element.737, ...), kind=kLoop, calls=%fused_computation.121.clone.1 | loop fusion | bytes 1048640 | tf_op jit(solution)/shard_map/while/body/eval_jaxpr/slice | solution.py:147
  57.3 2.8 %constant_dynamic-slice_fusion.65 = (f32[1,1,4096]{2,1,0:T(1,128)S(1)}, f32[1,1,4096]{2,1,0:T(1,128)S(1)}, f32[1,1,4096]{2,1,0:T(1,128)S(1)}, f32[1,1,4096]{2,1,...) fusion(f32[8,16,4096]{2,1,0:T(8,128)} %get-tuple-element.737, ...), kind=kLoop, calls=%fused_computation.121.clone.1 | loop fusion | bytes 1048640 | tf_op jit(solution)/shard_map/while/body/eval_jaxpr/slice | solution.py:147
  63.0 2.7 %constant_dynamic-slice_fusion.65 = (f32[1,1,4096]{2,1,0:T(1,128)S(1)}, f32[1,1,4096]{2,1,0:T(1,128)S(1)}, f32[1,1,4096]{2,1,0:T(1,128)S(1)}, f32[1,1,4096]{2,1,...) fusion(f32[8,16,4096]{2,1,0:T(8,128)} %get-tuple-element.737, ...), kind=kLoop, calls=%fused_computation.121.clone.1 | loop fusion | bytes 1048640 | tf_op jit(solution)/shard_map/while/body/eval_jaxpr/slice | solution.py:147
  68.6 2.8 %constant_dynamic-slice_fusion.65 = (f32[1,1,4096]{2,1,0:T(1,128)S(1)}, f32[1,1,4096]{2,1,0:T(1,128)S(1)}, f32[1,1,4096]{2,1,0:T(1,128)S(1)}, f32[1,1,4096]{2,1,...) fusion(f32[8,16,4096]{2,1,0:T(8,128)} %get-tuple-element.737, ...), kind=kLoop, calls=%fused_computation.121.clone.1 | loop fusion | bytes 1048640 | tf_op jit(solution)/shard_map/while/body/eval_jaxpr/slice | solution.py:147
  74.4 2.6 %constant_dynamic-slice_fusion.65 = (f32[1,1,4096]{2,1,0:T(1,128)S(1)}, f32[1,1,4096]{2,1,0:T(1,128)S(1)}, f32[1,1,4096]{2,1,0:T(1,128)S(1)}, f32[1,1,4096]{2,1,...) fusion(f32[8,16,4096]{2,1,0:T(8,128)} %get-tuple-element.737, ...), kind=kLoop, calls=%fused_computation.121.clone.1 | loop fusion | bytes 1048640 | tf_op jit(solution)/shard_map/while/body/eval_jaxpr/slice | solution.py:147
  79.8 2.8 %constant_dynamic-slice_fusion.65 = (f32[1,1,4096]{2,1,0:T(1,128)S(1)}, f32[1,1,4096]{2,1,0:T(1,128)S(1)}, f32[1,1,4096]{2,1,0:T(1,128)S(1)}, f32[1,1,4096]{2,1,...) fusion(f32[8,16,4096]{2,1,0:T(8,128)} %get-tuple-element.737, ...), kind=kLoop, calls=%fused_computation.121.clone.1 | loop fusion | bytes 1048640 | tf_op jit(solution)/shard_map/while/body/eval_jaxpr/slice | solution.py:147
  85.6 14.6 %all-gather.1 = bf16[32,4096]{1,0:T(8,128)(2,1)S(1)} all-gather(bf16[8,4096]{1,0:T(8,128)(2,1)S(1)} %convert_element_type.90), channel_id=3, replica_groups=mesh['pipe'=4,'ctx'=4,'tp'=2] {'ctx'}, dimensions={0}, use_global_device_ids=true | all-gather | bytes 327680 | tf_op jit(solution)/shard_map/all_gather | solution.py:18
  100.1 14.1 %all_gather.14 = bf16[4,8,4096]{2,1,0:T(8,128)(2,1)S(1)} all-gather(bf16[1,8,4096]{2,1,0:T(8,128)(2,1)S(1)} %get-tuple-element.408), channel_id=1, replica_groups=mesh['pipe'=4,'ctx'=4,'tp'=2] {'ctx'}, dimensions={0}, use_global_device_ids=true | all-gather | bytes 327680 | tf_op jit(solution)/shard_map/all_gather | solution.py:18
  114.5 8.6 %multiply_reduce_fusion.16 = f32[128,4096]{1,0:T(8,128)S(1)} fusion(f32[8,4096]{1,0:T(8,128)S(1)} %get-tuple-element.179, f32[128,4096]{1,0:T(8,128)} %reduce_window_sum.11, f32[8,4096]{1,0:T(8,128)S(1)} %get-tuple-element.785, f32[128,8]{1,0:T(8,128)S(1)} %bitcast.412), kind=kLoop, calls=%fused_computation.174 | loop fusion | flops 16252928 | bytes 4460544 | tf_op jit(solution)/shard_map/reduce_sum | solution.py:173
  123.2 1.8 %fusion.72 = bf16[128,4096]{1,0:T(8,128)(2,1)} fusion(bf16[128,4096]{1,0:T(8,128)(2,1)S(1)} %copy-done.2, f32[128,4096]{1,0:T(8,128)S(1)} %multiply_reduce_fusion.16, f32[8,16,4096]{2,1,0:T(8,128)S(1)} %copy-done.3, bf16[1,128,4096]{2,1,0:T(8,128)(2,1)S(1)} %copy-done.5, f32[4096]{0:T(1024)S(1)} %bitcast.415), kind=kLoop, calls=%fused_computation.184 | loop fusion | flops 5767168 | bytes 7356416 | tf_op jit(solution)/shard_map/convert_element_type | solution.py:182
  125.1 3.2 %conditional.2 = (f32[4,4,64]{2,1,0:T(4,128)S(1)}, f32[4,4,64,128]{3,2,1,0:T(8,128)S(1)}) conditional(s32[]{:T(128)} %bitcast.18, () %tuple.42, (s32[512]{0:T(512)S(1)}, s32[64]{0:T(128)S(1)}, bf16[2,512,4,128]{3,1,2,0:T(8,128)(2,1)}, bf16[1,128,16,128]{3,2,1,0:T(8,128)(2,1)S(1)}) %tuple.235), branch_computations={%region_0.0_spmd, %region_1.4_spmd} | conditional | flops 274234368 | bytes 14055724 | solution.py:71
  129.4 3.2 %conditional.3 = (f32[4,4,64]{2,1,0:T(4,128)S(1)}, f32[4,4,64,128]{3,2,1,0:T(8,128)S(1)}) conditional(s32[]{:T(128)} %bitcast.22, () %tuple.44, (s32[512]{0:T(512)S(1)}, s32[64]{0:T(128)S(1)}, bf16[2,512,4,128]{3,1,2,0:T(8,128)(2,1)}, bf16[1,128,16,128]{3,2,1,0:T(8,128)(2,1)S(1)}) %tuple.234), branch_computations={%region_4.5_spmd, %region_5.8_spmd} | conditional | flops 274234368 | bytes 14055724 | solution.py:71
  134.0 1.7 %collective-permute-start = (bf16[128,16,128]{2,1,0:T(8,128)(2,1)S(1)}, bf16[128,16,128]{2,1,0:T(8,128)(2,1)S(1)}, u32[]{:S(2)}, u32[]{:S(2)}) collective-permute-start(bf16[128,16,128]{2,1,0:T(8,128)(2,1)S(1)} %pad_maximum_fusion), channel_id=1, source_target_pairs={{24,0},{0,8},{8,16},{16,24},{25,1},{1,9},{9,17},{17,25},{26,2},{2,... | collective-permute-start | bytes 1572872 | tf_op jit(solution)/shard_map/ppermute | solution.py:38
  135.7 3.9 %collective-permute-done.2 = bf16[128,4096]{1,0:T(8,128)(2,1)} collective-permute-done((bf16[128,4096]{1,0:T(8,128)(2,1)}, bf16[128,4096]{1,0:T(8,128)(2,1)}, u32[]{:S(2)}, u32[]{:S(2)}) %collective-permute-start.2) | collective-permute-done | bytes 1048608 | tf_op jit(solution)/shard_map/ppermute | solution.py:38
  139.6 5.5 %collective-permute-done = bf16[128,16,128]{2,1,0:T(8,128)(2,1)S(1)} collective-permute-done((bf16[128,16,128]{2,1,0:T(8,128)(2,1)S(1)}, bf16[128,16,128]{2,1,0:T(8,128)(2,1)S(1)}, u32[]{:S(2)}, u32[]{:S(2)}) %collective-permute-start) | collective-permute-done | bytes 524320 | tf_op jit(solution)/shard_map/ppermute | solution.py:38
  145.9 2.3 %copy.71 = bf16[1,128,4096]{2,1,0:T(8,128)(2,1)} copy(bf16[1,128,4096]{2,1,0:T(8,128)(2,1)} %bitcast.48) | data formatting | bytes 2097152
  (141 shorter events, 41.8 us)
Async XLA Ops:
  7.2 15.3 %copy-start = (bf16[1,128,512]{2,1,0:T(8,128)(2,1)S(1)}, bf16[1,128,512]{2,1,0:T(8,128)(2,1)}, u32[]{:S(2)}) copy-start(bf16[1,128,512]{2,1,0:T(8,128)(2,1)} %param.24) | copy-start | bytes 393220
  7.2 117.9 %all-gather.4.cloned.1.call-start = ((), (), s32[]{:S(2)}) async-start(), calls=%async_computation | async-start | bytes 1310720 | tf_op jit(solution)/shard_map/all_gather | solution.py:99
  8.1 14.4 %copy-start.14 = (f32[1,4096]{1,0:T(1,128)S(1)}, f32[1,4096]{1,0:T(1,128)}, u32[]{:S(2)}) copy-start(f32[1,4096]{1,0:T(1,128)} %param.29) | copy-start | bytes 49156
  8.1 12.8 %collective-permute-start.1 = (bf16[3,4096]{1,0:T(4,128)(2,1)S(1)}, bf16[3,4096]{1,0:T(4,128)(2,1)S(1)}, u32[]{:S(2)}, u32[]{:S(2)}) collective-permute-start(bf16[3,4096]{1,0:T(4,128)(2,1)S(1)} %slice_bitcast_fusion), channel_id=1, source_target_pairs={{0,2},{2,4},{4,6},{1,3},{3,5},{5,7},{8,10},{10,12},{12,14},{9,11},... | collective-permute-start | bytes 73736 | tf_op jit(solution)/shard_map/ppermute | solution.py:12
  15.9 0.5 copy-start.12
  15.9 6.6 %copy-start.10 = (s32[64]{0:T(128)}, s32[64]{0:T(128)S(1)}, u32[]{:S(2)}) copy-start(s32[64]{0:T(128)S(1)} %iota_add_fusion) | copy-start | bytes 772
  29.3 4.0 %copy-start.1 = (bf16[128,4096]{1,0:T(8,128)(2,1)}, bf16[128,4096]{1,0:T(8,128)(2,1)S(1)}, u32[]{:S(2)}) copy-start(bf16[128,4096]{1,0:T(8,128)(2,1)S(1)} %get-tuple-element.306) | copy-start | bytes 3145732
  29.3 4.0 %copy-start.8 = (bf16[1,4096,16]{1,2,0:T(8,128)(2,1)S(1)}, bf16[1,4096,16]{1,2,0:T(8,128)(2,1)}, u32[]{:S(2)}) copy-start(bf16[1,4096,16]{1,2,0:T(8,128)(2,1)} %param.30) | copy-start | bytes 393220
  114.5 8.7 %copy-start.2 = (bf16[128,4096]{1,0:T(8,128)(2,1)S(1)}, bf16[128,4096]{1,0:T(8,128)(2,1)}, u32[]{:S(2)}) copy-start(bf16[128,4096]{1,0:T(8,128)(2,1)} %copy-done.1) | copy-start | bytes 3145732
  114.5 8.7 %copy-start.3 = (f32[8,16,4096]{2,1,0:T(8,128)S(1)}, f32[8,16,4096]{2,1,0:T(8,128)}, u32[]{:S(2)}) copy-start(f32[8,16,4096]{2,1,0:T(8,128)} %get-tuple-element.177) | copy-start | bytes 6291460
  114.5 8.7 %copy-start.5 = (bf16[1,128,4096]{2,1,0:T(8,128)(2,1)S(1)}, bf16[1,128,4096]{2,1,0:T(8,128)(2,1)}, u32[]{:S(2)}) copy-start(bf16[1,128,4096]{2,1,0:T(8,128)(2,1)} %param.23) | copy-start | bytes 3145732
  114.5 8.7 %copy-start.9 = (f32[1,4096]{1,0:T(1,128)S(1)}, f32[1,4096]{1,0:T(1,128)}, u32[]{:S(2)}) copy-start(f32[1,4096]{1,0:T(1,128)} %param.31) | copy-start | bytes 49156
  123.2 1.8 %copy-start.4 = (bf16[1,128,16,128]{3,2,1,0:T(8,128)(2,1)S(1)}, bf16[1,128,16,128]{3,2,1,0:T(8,128)(2,1)}, u32[]{:S(2)}) copy-start(bf16[1,128,16,128]{3,2,1,0:T(8,128)(2,1)} %param.20) | copy-start | bytes 1572868
  123.2 1.8 %copy-start.13 = (s32[64]{0:T(128)S(1)}, s32[64]{0:T(128)}, u32[]{:S(2)}) copy-start(s32[64]{0:T(128)} %copy-done.12) | copy-start | bytes 772
  125.0 14.5 %collective-permute-start.2 = (bf16[128,4096]{1,0:T(8,128)(2,1)}, bf16[128,4096]{1,0:T(8,128)(2,1)}, u32[]{:S(2)}, u32[]{:S(2)}) collective-permute-start(bf16[128,4096]{1,0:T(8,128)(2,1)} %fusion.72), channel_id=1, source_target_pairs={{24,0},{0,8},{8,16},{16,24},{25,1},{1,9},{9,17},{17,25},{26,2},{2,... | collective-permute-start | bytes 3145736 | tf_op jit(solution)/shard_map/ppermute | solution.py:38
  125.1 4.3 %copy-start.11 = (s32[64]{0:T(128)S(1)}, s32[64]{0:T(128)}, u32[]{:S(2)}) copy-start(s32[64]{0:T(128)} %copy-done.10) | copy-start | bytes 772
  125.2 1.9 %copy-start.6 = (bf16[2,512,4,128]{3,1,2,0:T(8,128)(2,1)S(1)}, bf16[2,512,4,128]{3,1,2,0:T(8,128)(2,1)}, u32[]{:S(2)}) copy-start(bf16[2,512,4,128]{3,1,2,0:T(8,128)(2,1)} %get-tuple-element.142) | copy-start | bytes 3145732 | tf_op jit(solution)/shard_map/cond
  129.5 1.9 %copy-start.7 = (bf16[2,512,4,128]{3,1,2,0:T(8,128)(2,1)S(1)}, bf16[2,512,4,128]{3,1,2,0:T(8,128)(2,1)}, u32[]{:S(2)}) copy-start(bf16[2,512,4,128]{3,1,2,0:T(8,128)(2,1)} %get-tuple-element.146) | copy-start | bytes 3145732 | tf_op jit(solution)/shard_map/cond
  134.0 11.1 %collective-permute-start = (bf16[128,16,128]{2,1,0:T(8,128)(2,1)S(1)}, bf16[128,16,128]{2,1,0:T(8,128)(2,1)S(1)}, u32[]{:S(2)}, u32[]{:S(2)}) collective-permute-start(bf16[128,16,128]{2,1,0:T(8,128)(2,1)S(1)} %pad_maximum_fusion), channel_id=1, source_target_pairs={{24,0},{0,8},{8,16},{16,24},{25,1},{1,9},{9,17},{17,25},{26,2},{2,... | collective-permute-start | bytes 1572872 | tf_op jit(solution)/shard_map/ppermute | solution.py:38
Sparse Core Ops, SparseCore 0:
  14.9 28.1 all-gather.3
where the time goes:
time: 156 us; the launch traced here: 155 us
  local copies, waits for them, and re-layouts  43.7 us (28%)
  blocking collectives  33.8 us (22%)
  other arithmetic  31.5 us (20%)
  between operations  17 us (11%)
  matrix products  12.2 us (8%)
  waiting for transfers between devices  9.41 us (6%)
  starting transfers between devices  6.64 us (4%)
    all_gather x2, blocking collectives, prefix(): lax.all_gather(a.astype(kind), axis)  28.7 us
    slice x8, local copies, waits for them, and re-layouts, run_block(): drive_rows[offset][None, :]  21.6 us
    reduce_sum x32, other arithmetic, run_block(): outputs.append(jnp.sum(read_rows[offset][:, None] * carry_state, axis=0))  12.5 us
    ppermute x2, waiting for transfers between devices, passed_along_2(): return lax.ppermute(block, axis, route)  9.39 us
    reduce_sum x1, other arithmetic, mamba_layer(): jnp.sum(read_map[:, :, None] * jnp.exp(-decay_rate[None] * elapsed[:, Non...  8.63 us
    dot_general x1, matrix products, mamba_layer(): jnp.dot(step_low, step_weight, preferred_element_type=jnp.float32)  6.74 us
    dynamic_update_slice x8, local copies, waits for them, and re-layouts, mamba_layer(): lax.scan(run_block, jnp.zeros((state_count, channels), jnp.float32), (blo...  5.85 us
    unnamed x31, local copies, waits for them, and re-layouts  5.53 us
  transfers between devices with their start and end apart: 4, of which 2 were waited for; matrix products, arithmetic and copies ran while one was open for 53% of the time, Pallas kernels for 0%

commit v1 on v0

v1 whole, which is shorter than its diff:
```python
import functools
import math

import jax
import jax.numpy as jnp
from jax import lax
from jax.experimental import pallas as pl
from jax.experimental.pallas import tpu as pltpu
from jax.sharding import PartitionSpec as P

F32 = jnp.float32
BF16 = jnp.bfloat16
MESH = pl.DeviceIdType.MESH
CHUNK = 32
HALO = 16


def nt_dot(a, b, precision=None):
    return lax.dot_general(
        a, b, (((1,), (1,)), ((), ())), precision=precision, preferred_element_type=F32
    )


def silu(v):
    return v / (1.0 + jnp.exp(-v))


def kernel(
    sizes,
    q_hbm,
    kv_hbm,
    x_hbm,
    gate_hbm,
    low_hbm,
    sw_hbm,
    bias_ref,
    decay_ref,
    cw_ref,
    cb_ref,
    ew_ref,
    skip_ref,
    att_out,
    mam_out,
    q_v,
    kv_v,
    x_v,
    gate_v,
    low_v,
    sw_v,
    kv_all,
    halo,
    pad_v,
    act_v,
    step_v,
    drive_v,
    y_v,
    h_v,
    ebc_v,
    rb_v,
    part_v,
    tp_in,
    hend_v,
    ent_v,
    dtot_v,
    chain_out,
    chain_in,
    att_stage,
    mam_stage,
    local_sem,
    halo_sem,
    kv_send,
    kv_recv,
    tp_send,
    tp_recv,
    chain_sem,
    att_sem,
    mam_send,
    mam_recv,
):
    nctx, ntp, npipe = sizes
    T, C = x_v.shape
    heads, _, D = q_v.shape
    kvh = kv_v.shape[0] // 2
    group = heads // kvh
    N = decay_ref.shape[0]
    taps = cw_ref.shape[0]
    W = h_v.shape[1]
    G = C // W
    B = pad_v.shape[1]

    me = lax.axis_index("ctx")
    tp = lax.axis_index("tp")
    pipe = lax.axis_index("pipe")
    nxt = lax.rem(pipe + 1, npipe)
    prv = lax.rem(pipe + npipe - 1, npipe)

    local = []
    for i, (src, dst) in enumerate(
        (
            (x_hbm, x_v),
            (low_hbm, low_v),
            (sw_hbm, sw_v),
            (kv_hbm, kv_v),
            (q_hbm, q_v),
            (gate_hbm, gate_v),
        )
    ):
        copy = pltpu.make_async_copy(src, dst, local_sem.at[i])
        copy.start()
        local.append(copy)
    x_copy, low_copy, sw_copy, kv_copy, q_copy, gate_copy = local

    barrier = pltpu.get_barrier_semaphore()
    for d in range(1, nctx):
        pl.semaphore_signal(
            barrier, inc=1, device_id={"ctx": lax.rem(me + d, nctx)}, device_id_type=MESH
        )
    for d in range(1, ntp):
        pl.semaphore_signal(
            barrier, inc=1, device_id={"tp": lax.rem(tp + d, ntp)}, device_id_type=MESH
        )
    pl.semaphore_signal(barrier, inc=1, device_id={"pipe": nxt}, device_id_type=MESH)
    pl.semaphore_signal(barrier, inc=1, device_id={"pipe": prv}, device_id_type=MESH)
    pl.semaphore_wait(barrier, nctx - 1 + ntp - 1 + 2)

    later = jnp.minimum(me + 1, nctx - 1)
    halo_copy = pltpu.make_async_remote_copy(
        src_ref=x_hbm.at[pl.ds(T - HALO, HALO)],
        dst_ref=halo,
        send_sem=halo_sem.at[0],
        recv_sem=halo_sem.at[1],
        device_id={"ctx": later},
        device_id_type=MESH,
    )

    @pl.when(me + 1 < nctx)
    def _():
        halo_copy.start()

    def kv_copy_to(d):
        return pltpu.make_async_remote_copy(
            src_ref=kv_hbm,
            dst_ref=kv_all.at[me],
            send_sem=kv_send.at[d - 1],
            recv_sem=kv_recv.at[me],
            device_id={"ctx": jnp.minimum(me + d, nctx - 1)},
            device_id_type=MESH,
        )

    for d in range(1, nctx):

        @pl.when(me + d < nctx)
        def _(d=d):
            kv_copy_to(d).start()

    x_copy.wait()

    @pl.when(me > 0)
    def _():
        halo_copy.wait_recv()

    @pl.when(me == 0)
    def _():
        halo[...] = jnp.zeros_like(halo)

    part_v[...] = jnp.zeros_like(part_v)

    @pl.loop(0, C // B)
    def _(b):
        lanes = pl.ds(pl.multiple_of(b * B, B), B)
        pad_v[0:HALO, :] = halo[:, lanes].astype(F32)
        pad_v[HALO:, :] = x_v[:, lanes].astype(F32)
        conv = cb_ref[:, lanes]
        for k in range(taps):
            conv = conv + cw_ref[k : k + 1, lanes] * pad_v[pl.ds(HALO - (taps - 1) + k, T), :]
        act = silu(conv).astype(BF16)
        act_v[:, lanes] = act
        part_v[...] += nt_dot(ew_ref[:, lanes], act)

    def tp_copy(d):
        return pltpu.make_async_remote_copy(
            src_ref=part_v,
            dst_ref=tp_in.at[tp],
            send_sem=tp_send.at[d - 1],
            recv_sem=tp_recv.at[tp],
            device_id={"tp": lax.rem(tp + d, ntp)},
            device_id_type=MESH,
        )

    for d in range(1, ntp):
        tp_copy(d).start()

    low_copy.wait()
    sw_copy.wait()

    @pl.loop(0, C // B)
    def _(b):
        lanes = pl.ds(pl.multiple_of(b * B, B), B)
        v = jnp.dot(low_v[...], sw_v[:, lanes], preferred_element_type=F32) + bias_ref[:, lanes]
        step = jnp.maximum(v, 0.0) + jnp.log1p(jnp.exp(-jnp.abs(v)))
        step_v[:, lanes] = step
        drive_v[:, lanes] = step * act_v[:, lanes].astype(F32)
        dtot_v[:, lanes] = jnp.exp(
            -decay_ref[:, lanes] * jnp.sum(step, axis=0, keepdims=True)
        )

    entry = part_v[...]
    for d in range(1, ntp):
        other = lax.rem(tp + d, ntp)
        pltpu.make_async_remote_copy(
            src_ref=part_v,
            dst_ref=tp_in.at[other],
            send_sem=tp_send.at[d - 1],
            recv_sem=tp_recv.at[other],
            device_id={"tp": other},
            device_id_type=MESH,
        ).wait_recv()
        entry = entry + tp_in[other]

    for t in range(T):
        ebc_v[t * N : (t + 1) * N, :] = jnp.broadcast_to(entry[:N, t : t + 1], (N, 128))
    hi = lax.Precision.HIGHEST
    rows = lax.broadcasted_iota(jnp.int32, (T, T), 0)
    cols = lax.broadcasted_iota(jnp.int32, (T, T), 1)
    by_pos = nt_dot((rows == cols).astype(F32), entry, hi)
    width = CHUNK * N
    srow = lax.broadcasted_iota(jnp.int32, (2 * N, width), 0)
    scol = lax.broadcasted_iota(jnp.int32, (2 * N, width), 1)
    pick = (srow == N + lax.rem(scol, N)).astype(F32)
    spread = jnp.dot(by_pos, pick, precision=hi, preferred_element_type=F32)
    mrow = lax.rem(lax.broadcasted_iota(jnp.int32, (T, width), 0), CHUNK)
    mcol = lax.div(lax.broadcasted_iota(jnp.int32, (T, width), 1), N)
    rb_v[...] = jnp.where(mrow == mcol, spread, 0.0).astype(BF16)

    def run(lanes, start, driven):
        rate = -decay_ref[:, lanes]

        def pair(i, h):
            both = []
            for k in range(8):
                t = i * 8 + k
                decay = jnp.exp(rate * step_v[pl.ds(t, 1), lanes])
                h = decay * h
                if driven:
                    e = ebc_v[pl.ds(pl.multiple_of(t * N, N), N), :]
                    h = h + jnp.concatenate([e] * (W // 128), axis=1) * drive_v[pl.ds(t, 1), lanes]
                both.append(h)
                if k % 2 == 1:
                    h_v[pl.ds(pl.multiple_of((t - 1) * N, 2 * N), 2 * N), :] = jnp.concatenate(
                        both, axis=0
                    ).astype(BF16)
                    both = []
            return h

        return lax.fori_loop(0, T // 8, pair, start)

    def read_out(k):
        return jnp.dot(
            rb_v[k * CHUNK : (k + 1) * CHUNK, :],
            h_v[k * width : (k + 1) * width, :],
            preferred_element_type=F32,
        )

    @pl.loop(0, G)
    def _(g):
        lanes = pl.ds(pl.multiple_of(g * W, W), W)
        hend_v[:, lanes] = run(lanes, jnp.zeros((N, W), F32), True)
        for k in range(T // CHUNK):
            part = slice(k * CHUNK, (k + 1) * CHUNK)
            y_v[part, lanes] = read_out(k) + skip_ref[:, lanes] * act_v[part, lanes].astype(F32)

    half = C // 2
    chain_copy = pltpu.make_async_remote_copy(
        src_ref=chain_out,
        dst_ref=chain_in,
        send_sem=chain_sem.at[0],
        recv_sem=chain_sem.at[1],
        device_id={"ctx": later},
        device_id_type=MESH,
    )

    @pl.when(me > 0)
    def _():
        chain_copy.wait_recv()
        for s in range(2):
            cols = slice(s * half, (s + 1) * half)
            ent_v[:, cols] = chain_in[...].astype(F32)[s * N : (s + 1) * N, :]

    @pl.when(me == 0)
    def _():
        ent_v[...] = jnp.zeros_like(ent_v)

    @pl.when(me + 1 < nctx)
    def _():
        out = dtot_v[...] * ent_v[...] + hend_v[...]
        chain_out[...] = jnp.concatenate([out[:, :half], out[:, half:]], axis=0).astype(BF16)
        chain_copy.start()

    kv_copy.wait()
    q_copy.wait()

    def kv_wait(j, carry):
        pltpu.make_async_remote_copy(
            src_ref=kv_hbm,
            dst_ref=kv_all.at[j],
            send_sem=kv_send.at[0],
            recv_sem=kv_recv.at[j],
            device_id={"ctx": later},
            device_id_type=MESH,
        ).wait_recv()
        return carry

    lax.fori_loop(0, me, kv_wait, 0)
    scale = 1.0 / math.sqrt(D)
    qrow = lax.rem(lax.broadcasted_iota(jnp.int32, (group * T, T), 0), T)
    kcol = lax.broadcasted_iota(jnp.int32, (group * T, T), 1)
    seen = kcol <= qrow
    for g in range(kvh):
        q = q_v[g * group : (g + 1) * group].reshape(group * T, D)
        s = jnp.where(seen, nt_dot(q, kv_v[g]) * scale, -1e30)
        top = jnp.max(s, axis=1, keepdims=True)
        p = jnp.exp(s - top)
        total = jnp.sum(p, axis=1, keepdims=True)
        acc = jnp.dot(p.astype(BF16), kv_v[kvh + g], preferred_element_type=F32)

        def block(j, carry, q=q, g=g):
            top, total, acc = carry
            s = nt_dot(q, kv_all[j, g]) * scale
            new = jnp.maximum(top, jnp.max(s, axis=1, keepdims=True))
            fade = jnp.exp(top - new)
            p = jnp.exp(s - new)
            total = total * fade + jnp.sum(p, axis=1, keepdims=True)
            acc = acc * fade + jnp.dot(
                p.astype(BF16), kv_all[j, kvh + g], preferred_element_type=F32
            )
            return new, total, acc

        top, total, acc = lax.fori_loop(0, me, block, (top, total, acc))
        att_stage[g * group : (g + 1) * group] = (acc / total).astype(BF16).reshape(group, T, D)

    att_copy = pltpu.make_async_remote_copy(
        src_ref=att_stage,
        dst_ref=att_out,
        send_sem=att_sem.at[0],
        recv_sem=att_sem.at[1],
        device_id={"pipe": nxt},
        device_id_type=MESH,
    )
    att_copy.start()

    gate_copy.wait()

    def mam_copy(g):
        lanes = pl.ds(pl.multiple_of(g * W, W), W)
        return pltpu.make_async_remote_copy(
            src_ref=mam_stage.at[:, lanes],
            dst_ref=mam_out.at[:, lanes],
            send_sem=mam_send.at[g],
            recv_sem=mam_recv.at[g],
            device_id={"pipe": nxt},
            device_id_type=MESH,
        )

    @pl.loop(0, G)
    def _(g):
        lanes = pl.ds(pl.multiple_of(g * W, W), W)

        @pl.when(me > 0)
        def _():
            run(lanes, ent_v[:, lanes], False)
            for k in range(T // CHUNK):
                part = slice(k * CHUNK, (k + 1) * CHUNK)
                y_v[part, lanes] += read_out(k)

        for k in range(T // CHUNK):
            part = slice(k * CHUNK, (k + 1) * CHUNK)
            gate = gate_v[part, lanes].astype(F32)
            mam_stage[part, lanes] = (y_v[part, lanes] * silu(gate)).astype(BF16)
        mam_copy(g).start()

    @pl.when(me + 1 < nctx)
    def _():
        halo_copy.wait_send()
        chain_copy.wait_send()

    for d in range(1, nctx):

        @pl.when(me + d < nctx)
        def _(d=d):
            kv_copy_to(d).wait_send()

    for d in range(1, ntp):
        tp_copy(d).wait_send()
    att_copy.wait()

    @pl.loop(0, G)
    def _(g):
        mam_copy(g).wait()


def per_device(
    sizes,
    queries,
    key_value,
    mamba_in,
    gate_in,
    step_low,
    step_weight,
    step_bias,
    decay_rate,
    conv_weight,
    conv_bias,
    state_weight,
    skip_gain,
):
    nctx, ntp, _ = sizes
    T, H, D = queries.shape[1:]
    kvh = key_value.shape[3]
    C = mamba_in.shape[2]
    R = step_low.shape[2]
    N = decay_rate.shape[1]
    W = min(1024, C // 2)
    B = 256
    q = jnp.transpose(queries[0], (1, 0, 2))
    kv = jnp.transpose(key_value[0], (0, 2, 1, 3)).reshape(2 * kvh, T, D)
    anywhere = pl.BlockSpec(memory_space=pl.ANY)
    vmem = pl.BlockSpec(memory_space=pltpu.VMEM)
    dma = pltpu.SemaphoreType.DMA
    att, mam = pl.pallas_call(
        functools.partial(kernel, sizes),
        out_shape=(
            jax.ShapeDtypeStruct((H, T, D), BF16),
            jax.ShapeDtypeStruct((T, C), BF16),
        ),
        in_specs=[anywhere] * 6 + [vmem] * 6,
        out_specs=(anywhere, anywhere),
        scratch_shapes=[
            pltpu.VMEM((H, T, D), BF16),
            pltpu.VMEM((2 * kvh, T, D), BF16),
            pltpu.VMEM((T, C), BF16),
            pltpu.VMEM((T, C), BF16),
            pltpu.VMEM((T, R), BF16),
            pltpu.VMEM((R, C), BF16),
            pltpu.VMEM((nctx, 2 * kvh, T, D), BF16),
            pltpu.VMEM((HALO, C), BF16),
            pltpu.VMEM((HALO + T, B), F32),
            pltpu.VMEM((T, C), BF16),
            pltpu.VMEM((T, C), F32),
            pltpu.VMEM((T, C), F32),
            pltpu.VMEM((T, C), F32),
            pltpu.VMEM((T * N, W), BF16),
            pltpu.VMEM((T * N, 128), F32),
            pltpu.VMEM((T, CHUNK * N), BF16),
            pltpu.VMEM((2 * N, T), F32),
            pltpu.VMEM((ntp, 2 * N, T), F32),
            pltpu.VMEM((N, C), F32),
            pltpu.VMEM((N, C), F32),
            pltpu.VMEM((N, C), F32),
            pltpu.VMEM((2 * N, C // 2), BF16),
            pltpu.VMEM((2 * N, C // 2), BF16),
            pltpu.VMEM((H, T, D), BF16),
            pltpu.VMEM((T, C), BF16),
            dma((6,)),
            dma((2,)),
            dma((max(1, nctx - 1),)),
            dma((nctx,)),
            dma((max(1, ntp - 1),)),
            dma((ntp,)),
            dma((2,)),
            dma((2,)),
            dma((C // W,)),
            dma((C // W,)),
        ],
        compiler_params=pltpu.CompilerParams(
            collective_id=0, has_side_effects=True, vmem_limit_bytes=50 * 2**20
        ),
    )(
        q,
        kv,
        mamba_in[0],
        gate_in[0],
        step_low[0],
        step_weight[0],
        step_bias,
        decay_rate[0],
        conv_weight[0],
        conv_bias,
        state_weight[0].T,
        skip_gain,
    )
    return jnp.transpose(att, (1, 0, 2))[None], mam[None]


def solution(mesh):
    sizes = (mesh.shape["ctx"], mesh.shape["tp"], mesh.shape["pipe"])
    return jax.shard_map(
        functools.partial(per_device, sizes),
        mesh=mesh,
        in_specs=(
            P("pipe", "ctx", "tp", None),
            P("pipe", None, "ctx", "tp", None),
            P("pipe", "ctx", "tp"),
            P("pipe", "ctx", "tp"),
            P("pipe", "ctx", None),
            P("pipe", None, "tp"),
            P("pipe", "tp"),
            P("pipe", None, "tp"),
            P("pipe", None, "tp"),
            P("pipe", "tp"),
            P("pipe", "tp", None),
            P("pipe", "tp"),
        ),
        out_specs=(P("pipe", "ctx", "tp", None), P("pipe", "ctx", "tp")),
        check_vma=False,
    )
```

time: 156 us -> 70.8 us (0.45)
  the two profiles are of different devices: /device:TPU:0 before, /device:TPU:24 now
where the time goes in v1:
time: 70.8 us; the launch traced here: 70.3 us
  Pallas kernels  58.4 us (82%)
  local copies, waits for them, and re-layouts  11.2 us (16%)
    pallas_call x1, Pallas kernels, per_device(): pl.pallas_call(functools.partial(kernel, sizes), out_shape=(jax.ShapeDtyp...  58.4 us
    unnamed x19, local copies, waits for them, and re-layouts  10.2 us

profile of v1, /device:TPU:24, one launch (start us, length us, event | category | flops | bytes accessed | tf_op | source)
XLA Modules:
  0.0 70.3 jit_solution(9894411873364987556)
XLA Ops:
  0.6 1.0 %copy.15 = bf16[2,4,128,128]{3,2,1,0:T(8,128)(2,1)S(1)} copy(bf16[2,4,128,128]{3,1,2,0:T(4,128)(2,1)} %bitcast.33) | data formatting | bytes 524288 | tf_op jit(solution)/shard_map/transpose | solution.py:425
  1.6 1.2 %copy.18 = bf16[1,128,16,128]{3,1,2,0:T(8,128)(2,1)S(1)} copy(bf16[1,128,16,128]{3,2,1,0:T(8,128)(2,1)} %param.12) | data formatting | bytes 1048576 | tf_op args[0]
  2.8 0.0 copy-start
  2.8 1.2 %copy-done = bf16[1,128,4096]{2,1,0:T(8,128)(2,1)S(1)} copy-done((bf16[1,128,4096]{2,1,0:T(8,128)(2,1)S(1)}, bf16[1,128,4096]{2,1,0:T(8,128)(2,1)}, u32[]{:S(2)}) %copy-start) | copy-done | bytes 1048600
  4.0 0.0 copy-start.1
  4.0 0.9 %copy-done.1 = bf16[1,128,512]{2,1,0:T(8,128)(2,1)S(1)} copy-done((bf16[1,128,512]{2,1,0:T(8,128)(2,1)S(1)}, bf16[1,128,512]{2,1,0:T(8,128)(2,1)}, u32[]{:S(2)}) %copy-start.1) | copy-done | bytes 131096
  4.9 0.0 copy-start.2
  4.9 0.9 %copy-done.2 = f32[1,8,4096]{2,1,0:T(8,128)S(1)} copy-done((f32[1,8,4096]{2,1,0:T(8,128)S(1)}, f32[1,8,4096]{2,1,0:T(8,128)}, u32[]{:S(2)}) %copy-start.2) | copy-done | bytes 131096
  5.8 0.0 copy-start.3
  5.8 0.9 %copy-done.3 = bf16[1,4096,16]{1,2,0:T(8,128)(2,1)S(1)} copy-done((bf16[1,4096,16]{1,2,0:T(8,128)(2,1)S(1)}, bf16[1,4096,16]{1,2,0:T(8,128)(2,1)}, u32[]{:S(2)}) %copy-start.3) | copy-done | bytes 131096
  6.7 0.0 copy-start.4
  6.7 0.8 %copy-done.4 = f32[1,4,4096]{2,1,0:T(4,128)S(1)} copy-done((f32[1,4,4096]{2,1,0:T(4,128)S(1)}, f32[1,4,4096]{2,1,0:T(4,128)}, u32[]{:S(2)}) %copy-start.4) | copy-done | bytes 65560
  7.6 0.0 copy-start.5
  7.6 0.7 %copy-done.5 = f32[1,4096]{1,0:T(1,128)S(1)} copy-done((f32[1,4096]{1,0:T(1,128)S(1)}, f32[1,4096]{1,0:T(1,128)}, u32[]{:S(2)}) %copy-start.5) | copy-done | bytes 16408
  8.3 0.0 copy-start.6
  8.3 0.7 %copy-done.6 = f32[1,4096]{1,0:T(1,128)S(1)} copy-done((f32[1,4096]{1,0:T(1,128)S(1)}, f32[1,4096]{1,0:T(1,128)}, u32[]{:S(2)}) %copy-start.6) | copy-done | bytes 16408
  9.0 0.0 copy-start.7
  9.0 0.7 %copy-done.7 = f32[1,4096]{1,0:T(1,128)S(1)} copy-done((f32[1,4096]{1,0:T(1,128)S(1)}, f32[1,4096]{1,0:T(1,128)}, u32[]{:S(2)}) %copy-start.7) | copy-done | bytes 16408
  9.7 58.4 %shard_map.131 = (bf16[16,128,128]{2,1,0:T(8,128)(2,1)S(1)}, bf16[128,4096]{1,0:T(8,128)(2,1)S(1)}) custom-call(bf16[16,128,128]{2,1,0:T(8,128)(2,1)S(1)} %bitcast.22, bf16[8,128,128]{2,1,0:T(8,128)(2,1)S(1)} %bitcast.25, bf16[128,4096]{1,0:T(8,128)(2,1)S(1)} %bitcast.24, bf16[128,4096]{1,0:T(8,128)(2,1)} %bitcast.32, bf16[128,512]{1,0:T(8,128)(2,1)S(1)} %bitcast.27, ...), custom_call_target="tpu_custom_call" | custom-call | tf_op jit(solution)/shard_map/pallas_call | solution.py:429
  68.2 1.1 %copy.16 = bf16[1,128,16,128]{3,2,1,0:T(8,128)(2,1)} copy(bf16[1,128,16,128]{3,1,2,0:T(8,128)(2,1)S(1)} %bitcast.26) | data formatting | bytes 1048576
  69.3 1.0 %copy.20 = bf16[1,128,4096]{2,1,0:T(8,128)(2,1)} copy(bf16[1,128,4096]{2,1,0:T(8,128)(2,1)S(1)} %bitcast.23) | data formatting | bytes 2097152
Async XLA Ops:
  2.8 1.2 %copy-start = (bf16[1,128,4096]{2,1,0:T(8,128)(2,1)S(1)}, bf16[1,128,4096]{2,1,0:T(8,128)(2,1)}, u32[]{:S(2)}) copy-start(bf16[1,128,4096]{2,1,0:T(8,128)(2,1)} %param.14) | copy-start | bytes 3145732
  4.0 0.9 %copy-start.1 = (bf16[1,128,512]{2,1,0:T(8,128)(2,1)S(1)}, bf16[1,128,512]{2,1,0:T(8,128)(2,1)}, u32[]{:S(2)}) copy-start(bf16[1,128,512]{2,1,0:T(8,128)(2,1)} %param.16) | copy-start | bytes 393220
  4.9 0.9 %copy-start.2 = (f32[1,8,4096]{2,1,0:T(8,128)S(1)}, f32[1,8,4096]{2,1,0:T(8,128)}, u32[]{:S(2)}) copy-start(f32[1,8,4096]{2,1,0:T(8,128)} %param.19) | copy-start | bytes 393220
  5.8 0.9 %copy-start.3 = (bf16[1,4096,16]{1,2,0:T(8,128)(2,1)S(1)}, bf16[1,4096,16]{1,2,0:T(8,128)(2,1)}, u32[]{:S(2)}) copy-start(bf16[1,4096,16]{1,2,0:T(8,128)(2,1)} %param.22) | copy-start | bytes 393220
  6.7 0.8 %copy-start.4 = (f32[1,4,4096]{2,1,0:T(4,128)S(1)}, f32[1,4,4096]{2,1,0:T(4,128)}, u32[]{:S(2)}) copy-start(f32[1,4,4096]{2,1,0:T(4,128)} %param.20) | copy-start | bytes 196612
  7.6 0.7 %copy-start.5 = (f32[1,4096]{1,0:T(1,128)S(1)}, f32[1,4096]{1,0:T(1,128)}, u32[]{:S(2)}) copy-start(f32[1,4096]{1,0:T(1,128)} %bias_ref.1) | copy-start | bytes 49156
  8.3 0.7 %copy-start.6 = (f32[1,4096]{1,0:T(1,128)S(1)}, f32[1,4096]{1,0:T(1,128)}, u32[]{:S(2)}) copy-start(f32[1,4096]{1,0:T(1,128)} %cb_ref.1) | copy-start | bytes 49156
  9.0 0.7 %copy-start.7 = (f32[1,4096]{1,0:T(1,128)S(1)}, f32[1,4096]{1,0:T(1,128)}, u32[]{:S(2)}) copy-start(f32[1,4096]{1,0:T(1,128)} %skip_ref.1) | copy-start | bytes 49156

commit v2 on v1

--- a/solution.py
+++ b/solution.py
@@ -22,7 +22,7 @@
 
 
 def silu(v):
-    return v / (1.0 + jnp.exp(-v))
+    return 0.5 * v * (1.0 + jnp.tanh(0.5 * v))
 
 
 def kernel(
@@ -33,12 +33,12 @@
     gate_hbm,
     low_hbm,
     sw_hbm,
-    bias_ref,
-    decay_ref,
-    cw_ref,
-    cb_ref,
-    ew_ref,
-    skip_ref,
+    bias_hbm,
+    decay_hbm,
+    cw_hbm,
+    cb_hbm,
+    ew_hbm,
+    skip_hbm,
     att_out,
     mam_out,
     q_v,
@@ -47,6 +47,12 @@
     gate_v,
     low_v,
     sw_v,
+    bias_ref,
+    decay_ref,
+    cw_ref,
+    cb_ref,
+    ew_ref,
+    skip_ref,
     kv_all,
     halo,
     pad_v,
@@ -72,8 +78,11 @@
     kv_recv,
     tp_send,
     tp_recv,
-    chain_sem,
+    chain_send,
+    chain_recv,
     att_sem,
+    over_send,
+    over_recv,
     mam_send,
     mam_recv,
 ):
@@ -98,17 +107,20 @@
     for i, (src, dst) in enumerate(
         (
             (x_hbm, x_v),
+            (cw_hbm, cw_ref),
+            (cb_hbm, cb_ref),
+            (ew_hbm, ew_ref),
             (low_hbm, low_v),
             (sw_hbm, sw_v),
-            (kv_hbm, kv_v),
-            (q_hbm, q_v),
+            (bias_hbm, bias_ref),
+            (decay_hbm, decay_ref),
+            (skip_hbm, skip_ref),
             (gate_hbm, gate_v),
         )
     ):
         copy = pltpu.make_async_copy(src, dst, local_sem.at[i])
         copy.start()
         local.append(copy)
-    x_copy, low_copy, sw_copy, kv_copy, q_copy, gate_copy = local
 
     barrier = pltpu.get_barrier_semaphore()
     for d in range(1, nctx):
@@ -137,23 +149,21 @@
     def _():
         halo_copy.start()
 
-    def kv_copy_to(d):
-        return pltpu.make_async_remote_copy(
-            src_ref=kv_hbm,
-            dst_ref=kv_all.at[me],
-            send_sem=kv_send.at[d - 1],
-            recv_sem=kv_recv.at[me],
-            device_id={"ctx": jnp.minimum(me + d, nctx - 1)},
-            device_id_type=MESH,
-        )
-
-    for d in range(1, nctx):
-
-        @pl.when(me + d < nctx)
-        def _(d=d):
-            kv_copy_to(d).start()
-
-    x_copy.wait()
+    over = []
+    for i, (src, dst) in enumerate(((kv_hbm, kv_v), (q_hbm, q_v))):
+        copy = pltpu.make_async_remote_copy(
+            src_ref=src,
+            dst_ref=dst,
+            send_sem=over_send.at[i],
+            recv_sem=over_recv.at[i],
+            device_id={"pipe": nxt},
+            device_id_type=MESH,
+        )
+        copy.start()
+        over.append(copy)
+
+    for copy in local[:4]:
+        copy.wait()
 
     @pl.when(me > 0)
     def _():
@@ -190,8 +200,26 @@
     for d in range(1, ntp):
         tp_copy(d).start()
 
-    low_copy.wait()
-    sw_copy.wait()
+    over[0].wait_recv()
+
+    def kv_copy_to(d):
+        return pltpu.make_async_remote_copy(
+            src_ref=kv_v,
+            dst_ref=kv_all.at[me],
+            send_sem=kv_send.at[d - 1],
+            recv_sem=kv_recv.at[me],
+            device_id={"ctx": jnp.minimum(me + d, nctx - 1)},
+            device_id_type=MESH,
+        )
+
+    for d in range(1, nctx):
+
+        @pl.when(me + d < nctx)
+        def _(d=d):
+            kv_copy_to(d).start()
+
+    for copy in local[4:9]:
+        copy.wait()
 
     @pl.loop(0, C // B)
     def _(b):
@@ -237,8 +265,8 @@
 
         def pair(i, h):
             both = []
-            for k in range(8):
-                t = i * 8 + k
+            for k in range(16):
+                t = i * 16 + k
                 decay = jnp.exp(rate * step_v[pl.ds(t, 1), lanes])
                 h = decay * h
                 if driven:
@@ -252,7 +280,7 @@
                     both = []
             return h
 
-        return lax.fori_loop(0, T // 8, pair, start)
+        return lax.fori_loop(0, T // 16, pair, start)
 
     def read_out(k):
         return jnp.dot(
@@ -260,6 +288,37 @@
             h_v[k * width : (k + 1) * width, :],
             preferred_element_type=F32,
         )
+
+    half = W // 2
+
+    def chain_copy(g):
+        return pltpu.make_async_remote_copy(
+            src_ref=chain_out.at[g],
+            dst_ref=chain_in.at[g],
+            send_sem=chain_send.at[g],
+            recv_sem=chain_recv.at[g],
+            device_id={"ctx": later},
+            device_id_type=MESH,
+        )
+
+    def hand_down(g):
+        lanes = pl.ds(pl.multiple_of(g * W, W), W)
+
+        @pl.when(me == 0)
+        def _():
+            ent_v[:, lanes] = jnp.zeros((N, W), F32)
+
+        @pl.when(me > 0)
+        def _():
+            chain_copy(g).wait_recv()
+            both = chain_in[g].astype(F32)
+            ent_v[:, lanes] = jnp.concatenate([both[:N], both[N:]], axis=1)
+
+        @pl.when(me + 1 < nctx)
+        def _():
+            out = dtot_v[:, lanes] * ent_v[:, lanes] + hend_v[:, lanes]
+            chain_out[g] = jnp.concatenate([out[:, :half], out[:, half:]], axis=0).astype(BF16)
+            chain_copy(g).start()
 
     @pl.loop(0, G)
     def _(g):
@@ -269,39 +328,56 @@
             part = slice(k * CHUNK, (k + 1) * CHUNK)
             y_v[part, lanes] = read_out(k) + skip_ref[:, lanes] * act_v[part, lanes].astype(F32)
 
-    half = C // 2
-    chain_copy = pltpu.make_async_remote_copy(
-        src_ref=chain_out,
-        dst_ref=chain_in,
-        send_sem=chain_sem.at[0],
-        recv_sem=chain_sem.at[1],
-        device_id={"ctx": later},
-        device_id_type=MESH,
-    )
-
-    @pl.when(me > 0)
-    def _():
-        chain_copy.wait_recv()
-        for s in range(2):
-            cols = slice(s * half, (s + 1) * half)
-            ent_v[:, cols] = chain_in[...].astype(F32)[s * N : (s + 1) * N, :]
-
-    @pl.when(me == 0)
-    def _():
-        ent_v[...] = jnp.zeros_like(ent_v)
-
-    @pl.when(me + 1 < nctx)
-    def _():
-        out = dtot_v[...] * ent_v[...] + hend_v[...]
-        chain_out[...] = jnp.concatenate([out[:, :half], out[:, half:]], axis=0).astype(BF16)
-        chain_copy.start()
-
-    kv_copy.wait()
-    q_copy.wait()
+        @pl.when(g >= me)
+        def _():
+            hand_down(g - me)
+
+    local[9].wait()
+
+    def mam_copy(g):
+        lanes = pl.ds(pl.multiple_of(g * W, W), W)
+        return pltpu.make_async_remote_copy(
+            src_ref=mam_stage.at[:, lanes],
+            dst_ref=mam_out.at[:, lanes],
+            send_sem=mam_send.at[g],
+            recv_sem=mam_recv.at[g],
+            device_id={"pipe": nxt},
+            device_id_type=MESH,
+        )
+
+    def finish(g):
+        lanes = pl.ds(pl.multiple_of(g * W, W), W)
+
+        @pl.when(me > 0)
+        def _():
+            run(lanes, ent_v[:, lanes], False)
+            for k in range(T // CHUNK):
+                part = slice(k * CHUNK, (k + 1) * CHUNK)
+                y_v[part, lanes] += read_out(k)
+
+        for k in range(T // CHUNK):
+            part = slice(k * CHUNK, (k + 1) * CHUNK)
+            gate = gate_v[part, lanes].astype(F32)
+            mam_stage[part, lanes] = (y_v[part, lanes] * silu(gate)).astype(BF16)
+        mam_copy(g).start()
+
+    lag = max(0, nctx - 1 - G)
+
+    @pl.loop(0, lag + G)
+    def _(i):
+        @pl.when((G + i >= me) & (i < me))
+        def _():
+            hand_down(G + i - me)
+
+        @pl.when(i >= lag)
+        def _():
+            finish(i - lag)
+
+    over[1].wait_recv()
 
     def kv_wait(j, carry):
         pltpu.make_async_remote_copy(
-            src_ref=kv_hbm,
+            src_ref=kv_v,
             dst_ref=kv_all.at[j],
             send_sem=kv_send.at[0],
             recv_sem=kv_recv.at[j],
@@ -338,50 +414,16 @@
         top, total, acc = lax.fori_loop(0, me, block, (top, total, acc))
         att_stage[g * group : (g + 1) * group] = (acc / total).astype(BF16).reshape(group, T, D)
 
-    att_copy = pltpu.make_async_remote_copy(
-        src_ref=att_stage,
-        dst_ref=att_out,
-        send_sem=att_sem.at[0],
-        recv_sem=att_sem.at[1],
-        device_id={"pipe": nxt},
-        device_id_type=MESH,
-    )
+    att_copy = pltpu.make_async_copy(att_stage, att_out, att_sem)
     att_copy.start()
-
-    gate_copy.wait()
-
-    def mam_copy(g):
-        lanes = pl.ds(pl.multiple_of(g * W, W), W)
-        return pltpu.make_async_remote_copy(
-            src_ref=mam_stage.at[:, lanes],
-            dst_ref=mam_out.at[:, lanes],
-            send_sem=mam_send.at[g],
-            recv_sem=mam_recv.at[g],
-            device_id={"pipe": nxt},
-            device_id_type=MESH,
-        )
-
-    @pl.loop(0, G)
-    def _(g):
-        lanes = pl.ds(pl.multiple_of(g * W, W), W)
-
-        @pl.when(me > 0)
-        def _():
-            run(lanes, ent_v[:, lanes], False)
-            for k in range(T // CHUNK):
-                part = slice(k * CHUNK, (k + 1) * CHUNK)
-                y_v[part, lanes] += read_out(k)
-
-        for k in range(T // CHUNK):
-            part = slice(k * CHUNK, (k + 1) * CHUNK)
-            gate = gate_v[part, lanes].astype(F32)
-            mam_stage[part, lanes] = (y_v[part, lanes] * silu(gate)).astype(BF16)
-        mam_copy(g).start()
 
     @pl.when(me + 1 < nctx)
     def _():
         halo_copy.wait_send()
-        chain_copy.wait_send()
+
+        @pl.loop(0, G)
+        def _(g):
+            chain_copy(g).wait_send()
 
     for d in range(1, nctx):
 
@@ -391,6 +433,8 @@
 
     for d in range(1, ntp):
         tp_copy(d).wait_send()
+    for copy in over:
+        copy.wait_send()
     att_copy.wait()
 
     @pl.loop(0, G)
@@ -424,7 +468,6 @@
     q = jnp.transpose(queries[0], (1, 0, 2))
     kv = jnp.transpose(key_value[0], (0, 2, 1, 3)).reshape(2 * kvh, T, D)
     anywhere = pl.BlockSpec(memory_space=pl.ANY)
-    vmem = pl.BlockSpec(memory_space=pltpu.VMEM)
     dma = pltpu.SemaphoreType.DMA
     att, mam = pl.pallas_call(
         functools.partial(kernel, sizes),
@@ -432,7 +475,7 @@
             jax.ShapeDtypeStruct((H, T, D), BF16),
             jax.ShapeDtypeStruct((T, C), BF16),
         ),
-        in_specs=[anywhere] * 6 + [vmem] * 6,
+        in_specs=[anywhere] * 12,
         out_specs=(anywhere, anywhere),
         scratch_shapes=[
             pltpu.VMEM((H, T, D), BF16),
@@ -441,6 +484,12 @@
             pltpu.VMEM((T, C), BF16),
             pltpu.VMEM((T, R), BF16),
             pltpu.VMEM((R, C), BF16),
+            pltpu.VMEM((1, C), F32),
+            pltpu.VMEM((N, C), F32),
+            pltpu.VMEM(conv_weight.shape[1:], F32),
+            pltpu.VMEM((1, C), F32),
+            pltpu.VMEM((2 * N, C), BF16),
+            pltpu.VMEM((1, C), F32),
             pltpu.VMEM((nctx, 2 * kvh, T, D), BF16),
             pltpu.VMEM((HALO, C), BF16),
             pltpu.VMEM((HALO + T, B), F32),
@@ -456,23 +505,26 @@
             pltpu.VMEM((N, C), F32),
             pltpu.VMEM((N, C), F32),
             pltpu.VMEM((N, C), F32),
-            pltpu.VMEM((2 * N, C // 2), BF16),
-            pltpu.VMEM((2 * N, C // 2), BF16),
+            pltpu.VMEM((C // W, 2 * N, W // 2), BF16),
+            pltpu.VMEM((C // W, 2 * N, W // 2), BF16),
             pltpu.VMEM((H, T, D), BF16),
             pltpu.VMEM((T, C), BF16),
-            dma((6,)),
+            dma((10,)),
             dma((2,)),
             dma((max(1, nctx - 1),)),
             dma((nctx,)),
             dma((max(1, ntp - 1),)),
             dma((ntp,)),
+            dma((C // W,)),
+            dma((C // W,)),
+            dma,
             dma((2,)),
             dma((2,)),
             dma((C // W,)),
             dma((C // W,)),
         ],
         compiler_params=pltpu.CompilerParams(
-            collective_id=0, has_side_effects=True, vmem_limit_bytes=50 * 2**20
+            collective_id=0, has_side_effects=True, vmem_limit_bytes=60 * 2**20
         ),
     )(
         q,

time: 70.8 us -> 63.5 us (0.90)
  Pallas kernels: 58.4 us -> 54.4 us
  local copies, waits for them, and re-layouts: 11.2 us -> 8.12 us
    pallas_call x1, Pallas kernels: 58.4 us -> 54.4 us  [per_device(): pl.pallas_call(functools.partial(kernel, sizes), out_shape=(jax.ShapeDtyp...]
    unnamed x19 -> x3, local copies, waits for them, and re-layouts: 10.2 us -> 6.43 us
where the time goes in v2:
time: 63.5 us; the launch traced here: 63.2 us
  Pallas kernels  54.4 us (86%)
  local copies, waits for them, and re-layouts  8.12 us (13%)
  between operations  0.64 us (1%)
    pallas_call x1, Pallas kernels, per_device(): pl.pallas_call(functools.partial(kernel, sizes), out_shape=(jax.ShapeDtyp...  54.4 us
    unnamed x3, local copies, waits for them, and re-layouts  6.43 us
    transpose x1, local copies, waits for them, and re-layouts, per_device(): kv = jnp.transpose(key_value[0], (0, 2, 1, 3)).reshape(2 * kvh, T, D)  1.69 us

profile of v2, /device:TPU:24, one launch (start us, length us, event | category | flops | bytes accessed | tf_op | source)
XLA Modules:
  0.0 63.2 jit_solution(14806229397081300019)
XLA Ops:
  0.6 1.7 %copy.15 = bf16[2,4,128,128]{3,2,1,0:T(8,128)(2,1)} copy(bf16[2,4,128,128]{3,1,2,0:T(4,128)(2,1)} %bitcast.29) | data formatting | bytes 524288 | tf_op jit(solution)/shard_map/transpose | solution.py:469
  2.3 2.0 %copy.18 = bf16[1,128,16,128]{3,1,2,0:T(8,128)(2,1)} copy(bf16[1,128,16,128]{3,2,1,0:T(8,128)(2,1)} %param.12) | data formatting | bytes 1048576 | tf_op args[0]
  4.3 54.4 %shard_map.131 = (bf16[16,128,128]{2,1,0:T(8,128)(2,1)}, bf16[128,4096]{1,0:T(8,128)(2,1)}) custom-call(bf16[16,128,128]{2,1,0:T(8,128)(2,1)} %bitcast.23, bf16[8,128,128]{2,1,0:T(8,128)(2,1)} %bitcast.27, bf16[128,4096]{1,0:T(8,128)(2,1)} %bitcast.25, bf16[128,4096]{1,0:T(8,128)(2,1)} %bitcast.26, bf16[128,512]{1,0:T(8,128)(2,1)} %bitcast.30, ...), custom_call_target="tpu_custom_call" | custom-call | tf_op jit(solution)/shard_map/pallas_call | solution.py:472
  58.7 2.2 %copy.16 = bf16[1,128,16,128]{3,2,1,0:T(8,128)(2,1)} copy(bf16[1,128,16,128]{3,1,2,0:T(8,128)(2,1)} %bitcast.28) | data formatting | bytes 1048576
  60.9 2.3 %copy.20 = bf16[1,128,4096]{2,1,0:T(8,128)(2,1)} copy(bf16[1,128,4096]{2,1,0:T(8,128)(2,1)} %bitcast.24) | data formatting | bytes 2097152

commit v3 on v2

--- a/solution.py
+++ b/solution.py
@@ -42,7 +42,8 @@
     att_out,
     mam_out,
     q_v,
-    kv_v,
+    score_v,
+    top_v,
     x_v,
     gate_v,
     low_v,
@@ -89,7 +90,7 @@
     nctx, ntp, npipe = sizes
     T, C = x_v.shape
     heads, _, D = q_v.shape
-    kvh = kv_v.shape[0] // 2
+    kvh = kv_all.shape[1] // 2
     group = heads // kvh
     N = decay_ref.shape[0]
     taps = cw_ref.shape[0]
@@ -150,7 +151,7 @@
         halo_copy.start()
 
     over = []
-    for i, (src, dst) in enumerate(((kv_hbm, kv_v), (q_hbm, q_v))):
+    for i, (src, dst) in enumerate(((kv_hbm, kv_all.at[me]), (q_hbm, q_v))):
         copy = pltpu.make_async_remote_copy(
             src_ref=src,
             dst_ref=dst,
@@ -162,6 +163,24 @@
         copy.start()
         over.append(copy)
 
+    def kv_copy(r):
+        j = jnp.maximum(me - r, 0)
+        return pltpu.make_async_remote_copy(
+            src_ref=kv_all.at[j],
+            dst_ref=kv_all.at[j],
+            send_sem=kv_send.at[r],
+            recv_sem=kv_recv.at[j],
+            device_id={"ctx": later},
+            device_id_type=MESH,
+        )
+
+    def kv_pass(r):
+        kv_copy(r).wait_recv()
+
+        @pl.when(me + 1 < nctx)
+        def _():
+            kv_copy(r).start()
+
     for copy in local[:4]:
         copy.wait()
 
@@ -172,6 +191,12 @@
     @pl.when(me == 0)
     def _():
         halo[...] = jnp.zeros_like(halo)
+
+    over[0].wait_recv()
+
+    @pl.when(me + 1 < nctx)
+    def _():
+        kv_copy(0).start()
 
     part_v[...] = jnp.zeros_like(part_v)
 
@@ -200,24 +225,6 @@
     for d in range(1, ntp):
         tp_copy(d).start()
 
-    over[0].wait_recv()
-
-    def kv_copy_to(d):
-        return pltpu.make_async_remote_copy(
-            src_ref=kv_v,
-            dst_ref=kv_all.at[me],
-            send_sem=kv_send.at[d - 1],
-            recv_sem=kv_recv.at[me],
-            device_id={"ctx": jnp.minimum(me + d, nctx - 1)},
-            device_id_type=MESH,
-        )
-
-    for d in range(1, nctx):
-
-        @pl.when(me + d < nctx)
-        def _(d=d):
-            kv_copy_to(d).start()
-
     for copy in local[4:9]:
         copy.wait()
 
@@ -231,6 +238,10 @@
         dtot_v[:, lanes] = jnp.exp(
             -decay_ref[:, lanes] * jnp.sum(step, axis=0, keepdims=True)
         )
+
+    @pl.when((me >= 1) & (me + 1 < nctx))
+    def _():
+        kv_pass(1)
 
     entry = part_v[...]
     for d in range(1, ntp):
@@ -332,6 +343,10 @@
         def _():
             hand_down(g - me)
 
+        @pl.when((g >= 1) & (g + 1 <= me) & (me + 1 < nctx))
+        def _():
+            kv_pass(g + 1)
+
     local[9].wait()
 
     def mam_copy(g):
@@ -375,44 +390,42 @@
 
     over[1].wait_recv()
 
-    def kv_wait(j, carry):
-        pltpu.make_async_remote_copy(
-            src_ref=kv_v,
-            dst_ref=kv_all.at[j],
-            send_sem=kv_send.at[0],
-            recv_sem=kv_recv.at[j],
-            device_id={"ctx": later},
-            device_id_type=MESH,
-        ).wait_recv()
-        return carry
-
-    lax.fori_loop(0, me, kv_wait, 0)
+    @pl.loop(jnp.where(me + 1 < nctx, G + 1, 1), me + 1)
+    def _(r):
+        kv_pass(r)
+
     scale = 1.0 / math.sqrt(D)
-    qrow = lax.rem(lax.broadcasted_iota(jnp.int32, (group * T, T), 0), T)
-    kcol = lax.broadcasted_iota(jnp.int32, (group * T, T), 1)
-    seen = kcol <= qrow
+    rows_of = lax.broadcasted_iota(jnp.int32, (group * T, T), 0)
+    seen = lax.broadcasted_iota(jnp.int32, (group * T, T), 1) <= lax.rem(rows_of, T)
+    ones = jnp.ones((T, 128), BF16)
+
+    def query(g):
+        return q_v[g * group : (g + 1) * group].reshape(group * T, D)
+
     for g in range(kvh):
-        q = q_v[g * group : (g + 1) * group].reshape(group * T, D)
-        s = jnp.where(seen, nt_dot(q, kv_v[g]) * scale, -1e30)
-        top = jnp.max(s, axis=1, keepdims=True)
-        p = jnp.exp(s - top)
-        total = jnp.sum(p, axis=1, keepdims=True)
-        acc = jnp.dot(p.astype(BF16), kv_v[kvh + g], preferred_element_type=F32)
-
-        def block(j, carry, q=q, g=g):
-            top, total, acc = carry
-            s = nt_dot(q, kv_all[j, g]) * scale
-            new = jnp.maximum(top, jnp.max(s, axis=1, keepdims=True))
-            fade = jnp.exp(top - new)
-            p = jnp.exp(s - new)
-            total = total * fade + jnp.sum(p, axis=1, keepdims=True)
-            acc = acc * fade + jnp.dot(
-                p.astype(BF16), kv_all[j, kvh + g], preferred_element_type=F32
-            )
-            return new, total, acc
-
-        top, total, acc = lax.fori_loop(0, me, block, (top, total, acc))
-        att_stage[g * group : (g + 1) * group] = (acc / total).astype(BF16).reshape(group, T, D)
+        s = jnp.where(seen, nt_dot(query(g), kv_all[me, g]), -1e30)
+        score_v[g, me] = s
+        top_v[g] = s
+
+    @pl.loop(0, me)
+    def _(j):
+        for g in range(kvh):
+            s = nt_dot(query(g), kv_all[j, g])
+            score_v[g, j] = s
+            top_v[g] = jnp.maximum(top_v[g], s)
+
+    for g in range(kvh):
+        top_v[g] = jnp.broadcast_to(jnp.max(top_v[g], axis=1, keepdims=True), (group * T, T))
+
+    def weigh(g, j):
+        p = jnp.exp((score_v[g, j] - top_v[g]) * scale).astype(BF16)
+        values = jnp.concatenate([kv_all[j, kvh + g], ones], axis=1)
+        return jnp.dot(p, values, preferred_element_type=F32)
+
+    for g in range(kvh):
+        acc = lax.fori_loop(0, me, lambda j, acc, g=g: acc + weigh(g, j), weigh(g, me))
+        out = (acc[:, :D] / acc[:, D:]).astype(BF16)
+        att_stage[g * group : (g + 1) * group] = out.reshape(group, T, D)
 
     att_copy = pltpu.make_async_copy(att_stage, att_out, att_sem)
     att_copy.start()
@@ -425,11 +438,11 @@
         def _(g):
             chain_copy(g).wait_send()
 
-    for d in range(1, nctx):
-
-        @pl.when(me + d < nctx)
-        def _(d=d):
-            kv_copy_to(d).wait_send()
+    @pl.when(me + 1 < nctx)
+    def _():
+        @pl.loop(0, me + 1)
+        def _(r):
+            kv_copy(r).wait_send()
 
     for d in range(1, ntp):
         tp_copy(d).wait_send()
@@ -479,7 +492,8 @@
         out_specs=(anywhere, anywhere),
         scratch_shapes=[
             pltpu.VMEM((H, T, D), BF16),
-            pltpu.VMEM((2 * kvh, T, D), BF16),
+            pltpu.VMEM((kvh, nctx, H // kvh * T, T), F32),
+            pltpu.VMEM((kvh, H // kvh * T, T), F32),
             pltpu.VMEM((T, C), BF16),
             pltpu.VMEM((T, C), BF16),
             pltpu.VMEM((T, R), BF16),
@@ -511,7 +525,7 @@
             pltpu.VMEM((T, C), BF16),
             dma((10,)),
             dma((2,)),
-            dma((max(1, nctx - 1),)),
+            dma((nctx,)),
             dma((nctx,)),
             dma((max(1, ntp - 1),)),
             dma((ntp,)),

time: 63.5 us -> 50.7 us (0.80)
  Pallas kernels: 54.4 us -> 41.6 us
    pallas_call x1, Pallas kernels: 54.4 us -> 41.6 us  [per_device(): pl.pallas_call(functools.partial(kernel, sizes), out_shape=(jax.ShapeDtyp...]
where the time goes in v3:
time: 50.7 us; the launch traced here: 50.4 us
  Pallas kernels  41.6 us (82%)
  local copies, waits for them, and re-layouts  8.12 us (16%)
  between operations  0.64 us (1%)
    pallas_call x1, Pallas kernels, per_device(): pl.pallas_call(functools.partial(kernel, sizes), out_shape=(jax.ShapeDtyp...  41.6 us
    unnamed x3, local copies, waits for them, and re-layouts  6.43 us
    transpose x1, local copies, waits for them, and re-layouts, per_device(): kv = jnp.transpose(key_value[0], (0, 2, 1, 3)).reshape(2 * kvh, T, D)  1.69 us

profile of v3, /device:TPU:24, one launch (start us, length us, event | category | flops | bytes accessed | tf_op | source)
XLA Modules:
  0.0 50.4 jit_solution(3522478236666033411)
XLA Ops:
  0.6 1.7 %copy.15 = bf16[2,4,128,128]{3,2,1,0:T(8,128)(2,1)} copy(bf16[2,4,128,128]{3,1,2,0:T(4,128)(2,1)} %bitcast.29) | data formatting | bytes 524288 | tf_op jit(solution)/shard_map/transpose | solution.py:482
  2.3 2.0 %copy.18 = bf16[1,128,16,128]{3,1,2,0:T(8,128)(2,1)} copy(bf16[1,128,16,128]{3,2,1,0:T(8,128)(2,1)} %param.12) | data formatting | bytes 1048576 | tf_op args[0]
  4.3 41.6 %shard_map.131 = (bf16[16,128,128]{2,1,0:T(8,128)(2,1)}, bf16[128,4096]{1,0:T(8,128)(2,1)}) custom-call(bf16[16,128,128]{2,1,0:T(8,128)(2,1)} %bitcast.23, bf16[8,128,128]{2,1,0:T(8,128)(2,1)} %bitcast.27, bf16[128,4096]{1,0:T(8,128)(2,1)} %bitcast.25, bf16[128,4096]{1,0:T(8,128)(2,1)} %bitcast.26, bf16[128,512]{1,0:T(8,128)(2,1)} %bitcast.30, ...), custom_call_target="tpu_custom_call" | custom-call | tf_op jit(solution)/shard_map/pallas_call | solution.py:485
  45.9 2.2 %copy.16 = bf16[1,128,16,128]{3,2,1,0:T(8,128)(2,1)} copy(bf16[1,128,16,128]{3,1,2,0:T(8,128)(2,1)} %bitcast.28) | data formatting | bytes 1048576
  48.1 2.3 %copy.20 = bf16[1,128,4096]{2,1,0:T(8,128)(2,1)} copy(bf16[1,128,4096]{2,1,0:T(8,128)(2,1)} %bitcast.24) | data formatting | bytes 2097152

commit v4 on v3

--- a/solution.py
+++ b/solution.py
@@ -13,6 +13,7 @@
 MESH = pl.DeviceIdType.MESH
 CHUNK = 32
 HALO = 16
+UNROLL = 16
 
 
 def nt_dot(a, b, precision=None):
@@ -233,8 +234,11 @@
         lanes = pl.ds(pl.multiple_of(b * B, B), B)
         v = jnp.dot(low_v[...], sw_v[:, lanes], preferred_element_type=F32) + bias_ref[:, lanes]
         step = jnp.maximum(v, 0.0) + jnp.log1p(jnp.exp(-jnp.abs(v)))
-        step_v[:, lanes] = step
-        drive_v[:, lanes] = step * act_v[:, lanes].astype(F32)
+        drive = step * act_v[:, lanes].astype(F32)
+        for i in range(B // 128):
+            cols = slice(i * 128, (i + 1) * 128)
+            step_v[b * (B // 128) + i] = step[:, cols]
+            drive_v[b * (B // 128) + i] = drive[:, cols]
         dtot_v[:, lanes] = jnp.exp(
             -decay_ref[:, lanes] * jnp.sum(step, axis=0, keepdims=True)
         )
@@ -271,27 +275,38 @@
     mcol = lax.div(lax.broadcasted_iota(jnp.int32, (T, width), 1), N)
     rb_v[...] = jnp.where(mrow == mcol, spread, 0.0).astype(BF16)
 
-    def run(lanes, start, driven):
+    tiles = W // 128
+
+    def run(group_at, start, driven):
+        lanes = pl.ds(pl.multiple_of(group_at * W, W), W)
         rate = -decay_ref[:, lanes]
-
-        def pair(i, h):
-            both = []
-            for k in range(16):
-                t = i * 16 + k
-                decay = jnp.exp(rate * step_v[pl.ds(t, 1), lanes])
-                h = decay * h
+        rates = [rate[:, c * 128 : (c + 1) * 128] for c in range(tiles)]
+
+        def turn(i, states):
+            states = list(states)
+            before = None
+            for k in range(UNROLL):
+                t = i * UNROLL + k
+                row = pl.ds(t, N, stride=0)
                 if driven:
                     e = ebc_v[pl.ds(pl.multiple_of(t * N, N), N), :]
-                    h = h + jnp.concatenate([e] * (W // 128), axis=1) * drive_v[pl.ds(t, 1), lanes]
-                both.append(h)
-                if k % 2 == 1:
-                    h_v[pl.ds(pl.multiple_of((t - 1) * N, 2 * N), 2 * N), :] = jnp.concatenate(
-                        both, axis=0
-                    ).astype(BF16)
-                    both = []
-            return h
-
-        return lax.fori_loop(0, T // 16, pair, start)
+                for c in range(tiles):
+                    at = group_at * tiles + c
+                    states[c] = jnp.exp(rates[c] * step_v[at, row, :]) * states[c]
+                    if driven:
+                        states[c] = states[c] + e * drive_v[at, row, :]
+                if k % 2 == 0:
+                    before = list(states)
+                else:
+                    for c in range(tiles):
+                        h_v[
+                            pl.ds(pl.multiple_of((t - 1) * N, 2 * N), 2 * N),
+                            c * 128 : (c + 1) * 128,
+                        ] = jnp.concatenate([before[c], states[c]], axis=0).astype(BF16)
+            return tuple(states)
+
+        start = tuple(start[:, c * 128 : (c + 1) * 128] for c in range(tiles))
+        return jnp.concatenate(lax.fori_loop(0, T // UNROLL, turn, start), axis=1)
 
     def read_out(k):
         return jnp.dot(
@@ -330,22 +345,6 @@
             out = dtot_v[:, lanes] * ent_v[:, lanes] + hend_v[:, lanes]
             chain_out[g] = jnp.concatenate([out[:, :half], out[:, half:]], axis=0).astype(BF16)
             chain_copy(g).start()
-
-    @pl.loop(0, G)
-    def _(g):
-        lanes = pl.ds(pl.multiple_of(g * W, W), W)
-        hend_v[:, lanes] = run(lanes, jnp.zeros((N, W), F32), True)
-        for k in range(T // CHUNK):
-            part = slice(k * CHUNK, (k + 1) * CHUNK)
-            y_v[part, lanes] = read_out(k) + skip_ref[:, lanes] * act_v[part, lanes].astype(F32)
-
-        @pl.when(g >= me)
-        def _():
-            hand_down(g - me)
-
-        @pl.when((g >= 1) & (g + 1 <= me) & (me + 1 < nctx))
-        def _():
-            kv_pass(g + 1)
 
     local[9].wait()
 
@@ -360,22 +359,42 @@
             device_id_type=MESH,
         )
 
-    def finish(g):
+    def leave(g):
         lanes = pl.ds(pl.multiple_of(g * W, W), W)
-
-        @pl.when(me > 0)
-        def _():
-            run(lanes, ent_v[:, lanes], False)
-            for k in range(T // CHUNK):
-                part = slice(k * CHUNK, (k + 1) * CHUNK)
-                y_v[part, lanes] += read_out(k)
-
         for k in range(T // CHUNK):
             part = slice(k * CHUNK, (k + 1) * CHUNK)
             gate = gate_v[part, lanes].astype(F32)
             mam_stage[part, lanes] = (y_v[part, lanes] * silu(gate)).astype(BF16)
         mam_copy(g).start()
 
+    @pl.loop(0, G)
+    def _(g):
+        lanes = pl.ds(pl.multiple_of(g * W, W), W)
+        hend_v[:, lanes] = run(g, jnp.zeros((N, W), F32), True)
+        for k in range(T // CHUNK):
+            part = slice(k * CHUNK, (k + 1) * CHUNK)
+            y_v[part, lanes] = read_out(k) + skip_ref[:, lanes] * act_v[part, lanes].astype(F32)
+
+        @pl.when(g >= me)
+        def _():
+            hand_down(g - me)
+
+        @pl.when(me == 0)
+        def _():
+            leave(g)
+
+        @pl.when((g >= 1) & (g + 1 <= me) & (me + 1 < nctx))
+        def _():
+            kv_pass(g + 1)
+
+    def finish(g):
+        lanes = pl.ds(pl.multiple_of(g * W, W), W)
+        run(g, ent_v[:, lanes], False)
+        for k in range(T // CHUNK):
+            part = slice(k * CHUNK, (k + 1) * CHUNK)
+            y_v[part, lanes] += read_out(k)
+        leave(g)
+
     lag = max(0, nctx - 1 - G)
 
     @pl.loop(0, lag + G)
@@ -384,7 +403,7 @@
         def _():
             hand_down(G + i - me)
 
-        @pl.when(i >= lag)
+        @pl.when((i >= lag) & (me > 0))
         def _():
             finish(i - lag)
 
@@ -398,6 +417,12 @@
     rows_of = lax.broadcasted_iota(jnp.int32, (group * T, T), 0)
     seen = lax.broadcasted_iota(jnp.int32, (group * T, T), 1) <= lax.rem(rows_of, T)
     ones = jnp.ones((T, 128), BF16)
+
+    def att_copy(g):
+        heads_of = pl.ds(g * group, group)
+        return pltpu.make_async_copy(
+            att_stage.at[heads_of], att_out.at[heads_of], att_sem.at[g]
+        )
 
     def query(g):
         return q_v[g * group : (g + 1) * group].reshape(group * T, D)
@@ -425,10 +450,9 @@
     for g in range(kvh):
         acc = lax.fori_loop(0, me, lambda j, acc, g=g: acc + weigh(g, j), weigh(g, me))
         out = (acc[:, :D] / acc[:, D:]).astype(BF16)
-        att_stage[g * group : (g + 1) * group] = out.reshape(group, T, D)
-
-    att_copy = pltpu.make_async_copy(att_stage, att_out, att_sem)
-    att_copy.start()
+        heads_of = slice(g * group, (g + 1) * group)
+        att_stage[heads_of] = out.reshape(group, T, D)
+        att_copy(g).start()
 
     @pl.when(me + 1 < nctx)
     def _():
@@ -448,7 +472,8 @@
         tp_copy(d).wait_send()
     for copy in over:
         copy.wait_send()
-    att_copy.wait()
+    for g in range(kvh):
+        att_copy(g).wait()
 
     @pl.loop(0, G)
     def _(g):
@@ -508,8 +533,8 @@
             pltpu.VMEM((HALO, C), BF16),
             pltpu.VMEM((HALO + T, B), F32),
             pltpu.VMEM((T, C), BF16),
-            pltpu.VMEM((T, C), F32),
-            pltpu.VMEM((T, C), F32),
+            pltpu.VMEM((C // 128, T, 128), F32),
+            pltpu.VMEM((C // 128, T, 128), F32),
             pltpu.VMEM((T, C), F32),
             pltpu.VMEM((T * N, W), BF16),
             pltpu.VMEM((T * N, 128), F32),
@@ -531,7 +556,7 @@
             dma((ntp,)),
             dma((C // W,)),
             dma((C // W,)),
-            dma,
+            dma((kvh,)),
             dma((2,)),
             dma((2,)),
             dma((C // W,)),

time: 50.7 us -> 49 us (0.966)
  Pallas kernels: 41.6 us -> 39.9 us
    pallas_call x1, Pallas kernels: 41.6 us -> 39.9 us  [per_device(): pl.pallas_call(functools.partial(kernel, sizes), out_shape=(jax.ShapeDtyp...]
where the time goes in v4:
time: 49 us; the launch traced here: 48.7 us
  Pallas kernels  39.9 us (81%)
  local copies, waits for them, and re-layouts  8.12 us (17%)
  between operations  0.64 us (1%)
    pallas_call x1, Pallas kernels, per_device(): pl.pallas_call(functools.partial(kernel, sizes), out_shape=(jax.ShapeDtyp...  39.9 us
    unnamed x3, local copies, waits for them, and re-layouts  6.43 us
    transpose x1, local copies, waits for them, and re-layouts, per_device(): kv = jnp.transpose(key_value[0], (0, 2, 1, 3)).reshape(2 * kvh, T, D)  1.69 us

profile of v4, /device:TPU:24, one launch (start us, length us, event | category | flops | bytes accessed | tf_op | source)
XLA Modules:
  0.0 48.7 jit_solution(14368549080236996517)
XLA Ops:
  0.6 1.7 %copy.15 = bf16[2,4,128,128]{3,2,1,0:T(8,128)(2,1)} copy(bf16[2,4,128,128]{3,1,2,0:T(4,128)(2,1)} %bitcast.29) | data formatting | bytes 524288 | tf_op jit(solution)/shard_map/transpose | solution.py:507
  2.3 2.0 %copy.18 = bf16[1,128,16,128]{3,1,2,0:T(8,128)(2,1)} copy(bf16[1,128,16,128]{3,2,1,0:T(8,128)(2,1)} %param.12) | data formatting | bytes 1048576 | tf_op args[0]
  4.3 39.9 %shard_map.131 = (bf16[16,128,128]{2,1,0:T(8,128)(2,1)}, bf16[128,4096]{1,0:T(8,128)(2,1)}) custom-call(bf16[16,128,128]{2,1,0:T(8,128)(2,1)} %bitcast.23, bf16[8,128,128]{2,1,0:T(8,128)(2,1)} %bitcast.27, bf16[128,4096]{1,0:T(8,128)(2,1)} %bitcast.25, bf16[128,4096]{1,0:T(8,128)(2,1)} %bitcast.26, bf16[128,512]{1,0:T(8,128)(2,1)} %bitcast.30, ...), custom_call_target="tpu_custom_call" | custom-call | tf_op jit(solution)/shard_map/pallas_call | solution.py:510
  44.2 2.2 %copy.16 = bf16[1,128,16,128]{3,2,1,0:T(8,128)(2,1)} copy(bf16[1,128,16,128]{3,1,2,0:T(8,128)(2,1)} %bitcast.28) | data formatting | bytes 1048576
  46.4 2.3 %copy.20 = bf16[1,128,4096]{2,1,0:T(8,128)(2,1)} copy(bf16[1,128,4096]{2,1,0:T(8,128)(2,1)} %bitcast.24) | data formatting | bytes 2097152

commit v5 on v4

--- a/solution.py
+++ b/solution.py
@@ -502,7 +502,7 @@
     R = step_low.shape[2]
     N = decay_rate.shape[1]
     W = min(1024, C // 2)
-    B = 256
+    B = min(512, C // 2)
     q = jnp.transpose(queries[0], (1, 0, 2))
     kv = jnp.transpose(key_value[0], (0, 2, 1, 3)).reshape(2 * kvh, T, D)
     anywhere = pl.BlockSpec(memory_space=pl.ANY)

time: 49 us -> 46.8 us (0.955)
  Pallas kernels: 39.9 us -> 37.7 us
    pallas_call x1, Pallas kernels: 39.9 us -> 37.7 us  [per_device(): pl.pallas_call(functools.partial(kernel, sizes), out_shape=(jax.ShapeDtyp...]
where the time goes in v5:
time: 46.8 us; the launch traced here: 46.5 us
  Pallas kernels  37.7 us (81%)
  local copies, waits for them, and re-layouts  8.12 us (17%)
  between operations  0.64 us (1%)
    pallas_call x1, Pallas kernels, per_device(): pl.pallas_call(functools.partial(kernel, sizes), out_shape=(jax.ShapeDtyp...  37.7 us
    unnamed x3, local copies, waits for them, and re-layouts  6.43 us
    transpose x1, local copies, waits for them, and re-layouts, per_device(): kv = jnp.transpose(key_value[0], (0, 2, 1, 3)).reshape(2 * kvh, T, D)  1.69 us

profile of v5, /device:TPU:24, one launch (start us, length us, event | category | flops | bytes accessed | tf_op | source)
XLA Modules:
  0.0 46.5 jit_solution(8197251922453104077)
XLA Ops:
  0.6 1.7 %copy.15 = bf16[2,4,128,128]{3,2,1,0:T(8,128)(2,1)} copy(bf16[2,4,128,128]{3,1,2,0:T(4,128)(2,1)} %bitcast.29) | data formatting | bytes 524288 | tf_op jit(solution)/shard_map/transpose | solution.py:507
  2.3 2.0 %copy.18 = bf16[1,128,16,128]{3,1,2,0:T(8,128)(2,1)} copy(bf16[1,128,16,128]{3,2,1,0:T(8,128)(2,1)} %param.12) | data formatting | bytes 1048576 | tf_op args[0]
  4.3 37.7 %shard_map.131 = (bf16[16,128,128]{2,1,0:T(8,128)(2,1)}, bf16[128,4096]{1,0:T(8,128)(2,1)}) custom-call(bf16[16,128,128]{2,1,0:T(8,128)(2,1)} %bitcast.23, bf16[8,128,128]{2,1,0:T(8,128)(2,1)} %bitcast.27, bf16[128,4096]{1,0:T(8,128)(2,1)} %bitcast.25, bf16[128,4096]{1,0:T(8,128)(2,1)} %bitcast.26, bf16[128,512]{1,0:T(8,128)(2,1)} %bitcast.30, ...), custom_call_target="tpu_custom_call" | custom-call | tf_op jit(solution)/shard_map/pallas_call | solution.py:510
  42.0 2.2 %copy.16 = bf16[1,128,16,128]{3,2,1,0:T(8,128)(2,1)} copy(bf16[1,128,16,128]{3,1,2,0:T(8,128)(2,1)} %bitcast.28) | data formatting | bytes 1048576
  44.2 2.3 %copy.20 = bf16[1,128,4096]{2,1,0:T(8,128)(2,1)} copy(bf16[1,128,4096]{2,1,0:T(8,128)(2,1)} %bitcast.24) | data formatting | bytes 2097152
